TPU v7x, 128 devices: a whole 4x4x4 slice. The times are simulated.
128 devices in a mesh: frame: 32 (over z, y_hi, x), head: 4 (over y_lo, core).
Axes of the slice: x: 4, y: 4 (y_hi: 2, y_lo: 2; y = y_hi * 2 + y_lo), z: 4, core: 2. Of those that a mesh axis runs over, the one named last changes fastest.
Arguments:
- latents: bfloat16 [36864, 3072], P(('frame', 'head')), may hold values from -6 to 6
- mod_shift: float32 [3072], replicated, may hold values from -3 to 3
- mod_scale: float32 [3072], replicated, may hold values from -3 to 3
- mod_gate: float32 [3072], replicated, may hold values from -4 to 4
- packed_weight: bfloat16 [3072, 9216], P(None, 'head'), may hold values from -0.109375 to 0.109375
- query_gain: float32 [128], replicated, may hold values from 0.8 to 2.2
- key_gain: float32 [128], replicated, may hold values from 0.8 to 2.2
- output_weight: bfloat16 [3072, 3072], P('head'), may hold values from -0.109375 to 0.109375
- cached: bfloat16 [36864, 3072], P('frame', 'head'), may hold values from -6 to 6
- active_tiles: int32 [32, 3], P('frame'), may hold values from 0 to 2, as said below
- active_count: int32 [32], P('frame'), may hold values from 1 to 3, as said below
- window_tiles: int32 [32, 3, 5], replicated, may hold values from 0 to 95, as said below
- window_count: int32 [32, 3], P('frame'), may hold values from 1 to 5, as said below
Outputs:
- block_output: bfloat16 [36864, 3072], P(('frame', 'head'))
Inputs may be any that keep to these rules, and one draw needn't show every extreme that they name: `active_tiles`: row g lists each of the group's 3 tile numbers once: first the active_count[g] active ones in increasing order, then the others in increasing order. `active_count`: at least one group has all 3 tiles active. `window_tiles`: entry [g, j, w] is a global tile number; the 5 entries of a row are distinct; every entry of group g, padding too, lies in group g - 1, g or g + 1, and over all entries of group g at most 2 distinct tiles of each neighbouring group occur. `window_count`: some live slot uses all 5 entries.
All inputs are finite; a program needn't handle non-finite values.
Results may differ from a plain program's by a relative error of at most 0.01.
Values may be sent and summed in bfloat16 or wider, within the bound.
A program may use at most 128 MiB of HBM per device.

v0:
```python
from functools import partial
import math

import jax
import jax.numpy as jnp
from jax import lax
from jax.sharding import PartitionSpec as P

HD = 128


def with_halo(block, sides, width):
    for axis, dim in sides:
        count = lax.axis_size(axis)
        forward = [(i, i + 1) for i in range(count - 1)]
        backward = [(target, source) for source, target in forward]
        low = lax.ppermute(
            lax.slice_in_dim(block, block.shape[dim] - width, None, axis=dim), axis, forward
        )
        high = lax.ppermute(lax.slice_in_dim(block, 0, width, axis=dim), axis, backward)
        block = jnp.concatenate([low, block, high], axis=dim)
    return block


def modulate(latent_rows, mod_shift, mod_scale):
    widened = latent_rows.astype(jnp.float32)
    centred = widened - jnp.mean(widened, axis=-1, keepdims=True)
    variance = jnp.mean(centred * centred, axis=-1, keepdims=True)
    return (centred * lax.rsqrt(variance + 1e-06) * (1.0 + mod_scale) + mod_shift).astype(
        jnp.bfloat16
    )


def head_norm(vectors, gain_vector):
    mean_square = jnp.mean(vectors * vectors, axis=-1, keepdims=True)
    return (vectors * lax.rsqrt(mean_square + 1e-06) * gain_vector).astype(jnp.bfloat16)


def key_step(position, running, slot_query, slot_keys, slot_count, key_bank, root_head):
    numerator, totals = running
    bank_entry = lax.dynamic_index_in_dim(key_bank, slot_keys[position], 0, keepdims=False)
    scores = (
        jnp.einsum("qhd,khd->hqk", slot_query, bank_entry[:, 0], preferred_element_type=jnp.float32)
        / root_head
    )
    weights = jnp.where(position < slot_count, jnp.exp(scores), 0.0)
    totals = totals + jnp.sum(weights, axis=-1)
    numerator = numerator + jnp.einsum(
        "hqk,khd->qhd",
        weights.astype(jnp.bfloat16),
        bank_entry[:, 1],
        preferred_element_type=jnp.float32,
    )
    return (numerator, totals)


def on_device(
    latents,
    mod_shift,
    mod_scale,
    mod_gate,
    packed_weight,
    query_gain,
    key_gain,
    output_weight,
    cached,
    active_tiles,
    active_count,
    window_tiles,
    window_count,
):
    tile_count = active_tiles.shape[1]
    window_len = window_tiles.shape[2]
    head_share = packed_weight.shape[1] // (3 * HD)
    share_width = head_share * HD
    slab_length = cached.shape[0]
    tile_rows = slab_length // tile_count
    group_index = lax.axis_index("frame")
    gathered = lax.all_gather(latents, "head", axis=0, tiled=True)
    normed = modulate(gathered, mod_shift, mod_scale)
    packed = jnp.dot(normed, packed_weight, preferred_element_type=jnp.float32).reshape(
        slab_length, head_share, 3, HD
    )
    queries = head_norm(packed[:, :, 0], query_gain).reshape(tile_count, tile_rows, head_share, HD)
    keys_here = head_norm(packed[:, :, 1], key_gain)
    values_here = packed[:, :, 2].astype(jnp.bfloat16)
    own_bank = jnp.stack([keys_here, values_here], axis=1).reshape(
        tile_count, tile_rows, 2, head_share, HD
    )
    window_rows = lax.dynamic_index_in_dim(window_tiles, group_index, 0, keepdims=False)
    key_bank = with_halo(own_bank, (("frame", 0),), tile_count)
    local_index = window_rows - (group_index - 1) * tile_count
    slot_tiles = active_tiles[0]
    live_slots = active_count[0]
    slot_counts = window_count[0]
    root_head = math.sqrt(HD)

    def slot_step(slot_index, results):
        slot_query = lax.dynamic_index_in_dim(queries, slot_tiles[slot_index], 0, keepdims=False)
        slot_keys = local_index[slot_index]
        slot_count = slot_counts[slot_index]
        initial = (
            jnp.zeros((tile_rows, head_share, HD), jnp.float32),
            jnp.zeros((head_share, tile_rows), jnp.float32),
        )
        stepper = partial(
            key_step,
            slot_query=slot_query,
            slot_keys=slot_keys,
            slot_count=slot_count,
            key_bank=key_bank,
            root_head=root_head,
        )
        numerator, totals = lax.fori_loop(0, window_len, stepper, initial)
        slot_out = (numerator / jnp.transpose(totals)[:, :, None]).astype(jnp.bfloat16)
        return lax.dynamic_update_index_in_dim(results, slot_out, slot_index, 0)

    blank_slots = jnp.zeros((tile_count, tile_rows, head_share, HD), jnp.bfloat16)
    results = lax.fori_loop(0, tile_count, slot_step, blank_slots)
    tile_ids = jnp.arange(tile_count, dtype=jnp.int32)
    placement = (slot_tiles[:, None] == tile_ids[None, :]) & (tile_ids < live_slots)[:, None]
    placed = jnp.einsum(
        "jt,jqc->tqc",
        placement.astype(jnp.bfloat16),
        results.reshape(tile_count, tile_rows, share_width),
        preferred_element_type=jnp.float32,
    )
    is_active = jnp.any(placement, axis=0)
    merged = jnp.where(
        is_active[:, None, None],
        placed.astype(jnp.bfloat16),
        cached.reshape(tile_count, tile_rows, share_width),
    ).reshape(slab_length, share_width)
    partial_out = jnp.dot(merged, output_weight, preferred_element_type=jnp.float32)
    summed = lax.psum_scatter(
        lax.optimization_barrier(partial_out.astype(jnp.bfloat16))
        .astype(jnp.float32)
        .astype(jnp.bfloat16),
        "head",
        scatter_dimension=0,
        tiled=True,
    ).astype(jnp.float32)
    return (latents.astype(jnp.float32) + mod_gate * summed).astype(jnp.bfloat16)


def solution(mesh):
    in_specs = (
        P(("frame", "head"), None),
        P(),
        P(),
        P(),
        P(None, "head"),
        P(),
        P(),
        P("head", None),
        P("frame", "head"),
        P("frame", None),
        P("frame"),
        P(),
        P("frame", None),
    )
    out_specs = P(("frame", "head"), None)
    return jax.shard_map(
        on_device, mesh=mesh, in_specs=in_specs, out_specs=out_specs, check_vma=False
    )
```

profile of v0, /device:TPU:104, one launch (start us, length us, event | category | flops | bytes accessed | tf_op | source)
XLA Modules:
  0.0 452.3 jit_solution(10627289364375538416)
XLA Ops:
  8.0 71.0 %all-gather.2.cloned.1.call-done = bf16[1152,3072]{1,0:T(8,128)(2,1)} async-done(((bf16[288,3072]{1,0:T(8,128)(2,1)}), bf16[1152,3072]{1,0:T(8,128)(2,1)}) %all-gather.2.cloned.1.call-update) | async-done | bytes 7077904 | tf_op jit(solution)/shard_map/all_gather | solution.py:79
  79.0 4.1 convert_reduce_fusion
  84.1 2.0 fusion.12
  86.1 25.8 %fusion.16 = f32[1152,2304]{0,1:T(8,128)} fusion(bf16[3072,2304]{1,0:T(8,128)(2,1)} %param.21, bf16[1152,3072]{1,0:T(8,128)(2,1)S(1)} %copy-done.2, f32[3072]{0:T(1024)S(1)} %copy-done.9, f32[3072]{0:T(1024)S(1)} %broadcast_add_fusion, f32[1152]{0:T(1024)S(1)} %add_rsqrt_fusion.2, f32[1152]{0:T(1024)S(1)} %broadcast_multiply_fusion), kind=kOutput, calls=%fused_computation.31 | convolution fusion | flops 16328687616 | bytes 31884288 | tf_op jit(solution)/shard_map/dot_general | solution.py:81
  111.9 2.2 slice.41
  114.1 7.5 %multiply_reduce_fusion = (f32[1152,6]{0,1:T(8,128)}, f32[1152,6]{0,1:T(8,128)}, f32[1152,6,1,128]{0,3,2,1:T(8,128)}, f32[1152,6,1,128]{0,3,2,1:T(8,128)}) fusion(f32[1152,6,3,128]{0,3,2,1:T(8,128)} %bitcast.91), kind=kLoop, calls=%fused_computation.40 | loop fusion | flops 3525120 | bytes 14211072 | tf_op jit(solution)/shard_map/reduce_sum | solution.py:35
  122.7 1.4 add_rsqrt_fusion
  124.8 5.2 %copy.38 = f32[1152,6,1,128]{3,0,1,2:T(8,128)} copy(f32[1152,6,1,128]{0,3,2,1:T(8,128)} %get-tuple-element.343) | data formatting | bytes 7077888 | tf_op jit(solution)/shard_map/slice | solution.py:85
  130.0 2.6 multiply_convert_fusion
  132.5 2.1 pad_maximum_fusion.1
  134.6 6.4 %collective-permute-start.1 = (bf16[3,384,2,6,128]{4,1,0,3,2:T(8,128)(2,1)}, bf16[3,384,2,6,128]{4,1,0,3,2:T(8,128)(2,1)}, u32[]{:S(2)}, u32[]{:S(2)}) collective-permute-start(bf16[3,384,2,6,128]{4,1,0,3,2:T(8,128)(2,1)} %pad_maximum_fusion.1), channel_id=1, source_target_pairs={{4,0},{8,4},{12,8},{16,12},{20,16},{24,20},{28,24},{32,28},{36,32}... | collective-permute-start | bytes 10616840 | tf_op jit(solution)/shard_map/ppermute | solution.py:20
  141.0 1.9 collective-permute-start
  145.1 1.4 fusion.25
  146.4 1.4 copy.37
  147.8 5.2 %copy.36 = f32[1152,6,1,128]{3,0,1,2:T(8,128)} copy(f32[1152,6,1,128]{0,3,2,1:T(8,128)} %get-tuple-element.344) | data formatting | bytes 7077888 | tf_op jit(solution)/shard_map/slice | solution.py:84
  153.0 3.5 multiply_convert_fusion.1
  156.5 61.4 %collective-permute-done.1 = bf16[3,384,2,6,128]{4,1,0,3,2:T(8,128)(2,1)} collective-permute-done((bf16[3,384,2,6,128]{4,1,0,3,2:T(8,128)(2,1)}, bf16[3,384,2,6,128]{4,1,0,3,2:T(8,128)(2,1)}, u32[]{:S(2)}, u32[]{:S(2)}) %collective-permute-start.1) | collective-permute-done | bytes 3538976 | tf_op jit(solution)/shard_map/ppermute | solution.py:20
  217.9 9.2 %collective-permute-done = bf16[3,384,2,6,128]{4,1,0,3,2:T(8,128)(2,1)} collective-permute-done((bf16[3,384,2,6,128]{4,1,0,3,2:T(8,128)(2,1)}, bf16[3,384,2,6,128]{4,1,0,3,2:T(8,128)(2,1)}, u32[]{:S(2)}, u32[]{:S(2)}) %collective-permute-start) | collective-permute-done | bytes 3538976 | tf_op jit(solution)/shard_map/ppermute | solution.py:17
  227.1 4.9 %pad_maximum_fusion = bf16[9,384,2,6,128]{4,1,0,3,2:T(8,128)(2,1)S(1)} fusion(bf16[3,384,2,6,128]{4,1,0,3,2:T(8,128)(2,1)} %collective-permute-done.1, bf16[3,384,1,6,128]{4,1,0,3,2:T(8,128)(2,1)S(1)} %bitcast.86, bf16[3,384,1,6,128]{4,1,0,3,2:T(8,128)(2,1)S(1)} %multiply_convert_fusion, bf16[3,384,2,6,128]{4,1,0,3,2:T(8,128)(2,1)} %collective-permute-done), kind=kLoop, calls=%fused_computation.30 | loop fusion | flops 15925248 | bytes 21233664 | tf_op jit(solution)/shard_map/concatenate | solution.py:21
  232.0 5.1 %copy.42 = bf16[9,384,2,6,128]{4,1,3,2,0:T(8,128)(2,1)} copy(bf16[9,384,2,6,128]{4,1,0,3,2:T(8,128)(2,1)S(1)} %pad_maximum_fusion) | data formatting | bytes 21233664 | tf_op jit(solution)/shard_map/while | solution.py:119
  237.1 119.8 %while.46 = (s32[]{:T(128)}, bf16[3,384,6,128]{1,3,2,0:T(8,128)(2,1)S(1)}, s32[3,5]{1,0:T(4,128)S(1)}, s32[3]{0:T(128)}, bf16[3,384,6,128]{3,1,0,2:T(8,128)(2,1)...) while((s32[]{:T(128)}, ...), condition=%wide.region_9.10_spmd, body=%wide.region_5.9_spmd.sunk | while | flops 459475200 | bytes 16564736 | solution.py:119
  237.1 1.2 dynamic_slice.66
  243.1 33.8 %while.47 = (s32[]{:T(128)}, f32[384,6,128]{0,2,1:T(8,128)S(1)}, f32[6,384]{1,0:T(8,128)S(1)}, s32[5]{0:T(128)}, bf16[9,384,2,6,128]{4,1,3,2,0:T(8,128)(2,1)}, /...) while((s32[]{:T(128)}, f32[384,6,128]{0,2,1:T(8,128)S(1)}, ...), condition=%wide.region_8.8_spmd.clone, body=%wide.region_6.7_spmd.clone.sunk | while | flops 458885376 | bytes 13602997 | solution.py:114
  246.5 1.4 dynamic-slice_bitcast_fusion.5
  253.3 1.4 dynamic-slice_bitcast_fusion.5
  260.0 1.4 dynamic-slice_bitcast_fusion.5
  266.8 1.4 dynamic-slice_bitcast_fusion.5
  273.5 1.4 dynamic-slice_bitcast_fusion.5
  277.0 1.3 dynamic_slice.66
  280.2 1.2 dynamic_slice.65
  283.0 33.8 %while.47 = (s32[]{:T(128)}, f32[384,6,128]{0,2,1:T(8,128)S(1)}, f32[6,384]{1,0:T(8,128)S(1)}, s32[5]{0:T(128)}, bf16[9,384,2,6,128]{4,1,3,2,0:T(8,128)(2,1)}, /...) while((s32[]{:T(128)}, f32[384,6,128]{0,2,1:T(8,128)S(1)}, ...), condition=%wide.region_8.8_spmd.clone, body=%wide.region_6.7_spmd.clone.sunk | while | flops 458885376 | bytes 13602997 | solution.py:114
  286.5 1.4 dynamic-slice_bitcast_fusion.5
  293.2 1.4 dynamic-slice_bitcast_fusion.5
  300.0 1.4 dynamic-slice_bitcast_fusion.5
  306.7 1.4 dynamic-slice_bitcast_fusion.5
  313.5 1.4 dynamic-slice_bitcast_fusion.5
  317.0 1.3 dynamic_slice.66
  322.9 33.8 %while.47 = (s32[]{:T(128)}, f32[384,6,128]{0,2,1:T(8,128)S(1)}, f32[6,384]{1,0:T(8,128)S(1)}, s32[5]{0:T(128)}, bf16[9,384,2,6,128]{4,1,3,2,0:T(8,128)(2,1)}, /...) while((s32[]{:T(128)}, f32[384,6,128]{0,2,1:T(8,128)S(1)}, ...), condition=%wide.region_8.8_spmd.clone, body=%wide.region_6.7_spmd.clone.sunk | while | flops 458885376 | bytes 13602997 | solution.py:114
  326.4 1.4 dynamic-slice_bitcast_fusion.5
  333.1 1.4 dynamic-slice_bitcast_fusion.5
  339.9 1.4 dynamic-slice_bitcast_fusion.5
  346.7 1.4 dynamic-slice_bitcast_fusion.5
  353.4 1.4 dynamic-slice_bitcast_fusion.5
  358.1 4.0 copy.43
  362.1 3.9 copy_select_fusion
  366.3 10.2 %convolution_convert_fusion = bf16[1152,3072]{1,0:T(8,128)(2,1)} fusion(bf16[1152,768]{1,0:T(8,128)(2,1)S(1)} %bitcast.93, bf16[768,3072]{1,0:T(8,128)(2,1)} %param.24), kind=kOutput, calls=%fused_computation.29 | convolution fusion | flops 5439356928 | bytes 13565952 | tf_op jit(solution)/shard_map/dot_general | solution.py:134
  376.5 65.5 %reduce-scatter.2.cloned.1.call-done = bf16[288,3072]{1,0:T(8,128)(2,1)} async-done(((bf16[1152,3072]{1,0:T(8,128)(2,1)}), bf16[288,3072]{1,0:T(8,128)(2,1)}) %reduce-scatter.2.cloned.1.call-update) | async-done | bytes 1769488 | tf_op jit(solution)/shard_map/reduce_scatter | solution.py:135
  442.1 3.4 add_convert_fusion
  (118 shorter events, 61.8 us)
Async XLA Ops:
  6.5 137.0 %copy-start = (s32[32,3,5]{0,1,2:T(4,128)S(1)}, s32[32,3,5]{0,1,2:T(4,128)}, u32[]{:S(2)}) copy-start(s32[32,3,5]{0,1,2:T(4,128)} %param.28) | copy-start | bytes 5764
  6.5 72.5 %all-gather.2.cloned.1.call-start = ((), (), s32[]{:S(2)}) async-start(), calls=%async_computation.1 | async-start | bytes 8847360 | tf_op jit(solution)/shard_map/all_gather | solution.py:79
  7.3 434.8 %reduce-scatter.2.cloned.1.call-start = ((), (), s32[]{:S(2)}) async-start(), calls=%async_computation.2 | async-start | bytes 8847360 | tf_op jit(solution)/shard_map/reduce_scatter | solution.py:135
  79.0 5.0 %copy-start.2 = (bf16[1152,3072]{1,0:T(8,128)(2,1)S(1)}, bf16[1152,3072]{1,0:T(8,128)(2,1)}, u32[]{:S(2)}) copy-start(bf16[1152,3072]{1,0:T(8,128)(2,1)} %all-gather.2.cloned.1.call-done) | copy-start | bytes 21233668
  84.1 2.0 copy-start.9
  124.8 5.2 %copy-start.7 = (f32[128]{0:T(128)S(1)}, f32[128]{0:T(128)}, u32[]{:S(2)}) copy-start(f32[128]{0:T(128)} %param.23) | copy-start | bytes 1540
  134.6 83.3 %collective-permute-start.1 = (bf16[3,384,2,6,128]{4,1,0,3,2:T(8,128)(2,1)}, bf16[3,384,2,6,128]{4,1,0,3,2:T(8,128)(2,1)}, u32[]{:S(2)}, u32[]{:S(2)}) collective-permute-start(bf16[3,384,2,6,128]{4,1,0,3,2:T(8,128)(2,1)} %pad_maximum_fusion.1), channel_id=1, source_target_pairs={{4,0},{8,4},{12,8},{16,12},{20,16},{24,20},{28,24},{32,28},{36,32}... | collective-permute-start | bytes 10616840 | tf_op jit(solution)/shard_map/ppermute | solution.py:20
  141.0 86.1 %collective-permute-start = (bf16[3,384,2,6,128]{4,1,0,3,2:T(8,128)(2,1)}, bf16[3,384,2,6,128]{4,1,0,3,2:T(8,128)(2,1)}, u32[]{:S(2)}, u32[]{:S(2)}) collective-permute-start(bf16[3,384,2,6,128]{4,1,0,3,2:T(8,128)(2,1)} %pad_maximum_fusion.1), channel_id=1, source_target_pairs={{0,4},{4,8},{8,12},{12,16},{16,20},{20,24},{24,28},{28,32},{32,36}... | collective-permute-start | bytes 10616840 | tf_op jit(solution)/shard_map/ppermute | solution.py:17
  145.1 7.9 %copy-start.10 = (pred[3]{0:T(512)(128)(4,1)}, pred[3]{0:T(512)(128)(4,1)S(1)}, u32[]{:S(2)}) copy-start(pred[3]{0:T(512)(128)(4,1)S(1)} %iota_compare_fusion.1) | copy-start | bytes 13
  147.8 5.2 %copy-start.8 = (f32[128]{0:T(128)S(1)}, f32[128]{0:T(128)}, u32[]{:S(2)}) copy-start(f32[128]{0:T(128)} %param.22) | copy-start | bytes 1540
  232.0 5.1 %copy-start.4 = (bf16[3,384,6,128]{1,3,2,0:T(8,128)(2,1)S(1)}, bf16[3,384,6,128]{1,3,2,0:T(8,128)(2,1)}, u32[]{:S(2)}) copy-start(bf16[3,384,6,128]{1,3,2,0:T(8,128)(2,1)} %custom-call.2) | copy-start | bytes 5308420
  356.9 1.2 copy-start.5
  356.9 5.2 %copy-start.11 = (pred[3]{0:T(512)(128)(4,1)S(1)}, pred[3]{0:T(512)(128)(4,1)}, u32[]{:S(2)}) copy-start(pred[3]{0:T(512)(128)(4,1)} %copy-done.10) | copy-start | bytes 13
  356.9 5.2 %copy-start.12 = (pred[3]{0:T(512)(128)(4,1)S(1)}, pred[3]{0:T(512)(128)(4,1)}, u32[]{:S(2)}) copy-start(pred[3]{0:T(512)(128)(4,1)} %fusion.25) | copy-start | bytes 13
  376.5 65.6 %copy-start.3 = (bf16[288,3072]{1,0:T(8,128)(2,1)S(1)}, bf16[288,3072]{1,0:T(8,128)(2,1)}, u32[]{:S(2)}) copy-start(bf16[288,3072]{1,0:T(8,128)(2,1)} %param.17) | copy-start | bytes 5308420
  376.5 65.6 %copy-start.6 = (f32[3072]{0:T(1024)S(1)}, f32[3072]{0:T(1024)}, u32[]{:S(2)}) copy-start(f32[3072]{0:T(1024)} %param.20) | copy-start | bytes 36868
  376.5 68.9 %copy-start.1 = (s32[32,3,5]{0,1,2:T(4,128)S(1)}, s32[32,3,5]{0,1,2:T(4,128)}, u32[]{:S(2)}) copy-start(s32[32,3,5]{0,1,2:T(4,128)} %param.28) | copy-start | bytes 5764
Sparse Core Ops, SparseCore 0:
  9.0 69.9 all-gather.1
  376.6 65.3 reduce-scatter.1
where the time goes:
time: 458 us; the launch traced here: 452 us
  waiting for transfers between devices  208 us (45%)
  local copies, waits for them, and re-layouts  79.1 us (17%)
  matrix products  68.8 us (15%)
  loops' own time  39.8 us (9%)
  other arithmetic  34.1 us (7%)
  between operations  14.2 us (3%)
  starting transfers between devices  8.35 us (2%)
    all_gather x1, waiting for transfers between devices, on_device(): gathered = lax.all_gather(latents, 'head', axis=0, tiled=True)  71 us
    reduce_scatter x1, waiting for transfers between devices, on_device(): lax.psum_scatter(lax.optimization_barrier(partial_out.astype(jnp.bfloat16...  65.5 us
    ppermute x1, waiting for transfers between devices, with_halo(): lax.ppermute(lax.slice_in_dim(block, 0, width, axis=dim), axis, backward)  61.4 us
    another operation x3, loops' own time, slot_step(): numerator, totals = lax.fori_loop(0, window_len, stepper, initial)  34.1 us
    dot_general x1, matrix products, on_device(): jnp.dot(normed, packed_weight, preferred_element_type=jnp.float32)  25.8 us
    squeeze x15, local copies, waits for them, and re-layouts, key_step(): lax.dynamic_index_in_dim(key_bank, slot_keys[position], 0, keepdims=False)  20.3 us
    dynamic_slice x15, local copies, waits for them, and re-layouts, key_step(): slot_keys[position]  18 us
    dot_general x15, matrix products, key_step(): jnp.einsum('hqk,khd->qhd', weights.astype(jnp.bfloat16), bank_entry[:, 1]...  16.7 us
  transfers between devices with their start and end apart: 4, of which 4 were waited for; matrix products, arithmetic and copies ran while one was open for 3% of the time, Pallas kernels for 0%

commit v1 on v0

v1 whole, which is shorter than its diff:
```python
import functools
import math

import jax
import jax.numpy as jnp
from jax import lax
from jax.experimental import pallas as pl
from jax.experimental.pallas import tpu as pltpu
from jax.sharding import PartitionSpec as P

HD = 128
BF16 = jnp.bfloat16
F32 = jnp.float32
MESH = pl.DeviceIdType.MESH


def kernel(
    sizes,
    latents_hbm,
    shift_ref,
    scale_ref,
    gate_ref,
    weight_hbm,
    query_gain_ref,
    key_gain_ref,
    out_weight_hbm,
    cached_hbm,
    active_tiles_ref,
    active_count_ref,
    window_tiles_ref,
    window_count_ref,
    out_hbm,
    latents,
    near,
    far,
    weight,
    queries,
    bank,
    rim_send,
    rim,
    numerator,
    totals,
    attended,
    out_weight,
    sib_sums,
    cross_sums,
    masks,
    local_sem,
    near_sib_send,
    near_sib_recv,
    cross_send,
    cross_recv,
    pass_send,
    pass_recv,
    rim_send_sem,
    rim_recv_sem,
    sums_send,
    sums_recv,
    last_send,
    last_recv,
):
    groups, heads, tile, width, window = sizes
    share = heads * HD
    chunk = tile // 4
    rows = 3 * chunk
    g = lax.axis_index("frame")
    h = lax.axis_index("head")
    y = h // 2
    c = h % 2
    sibling = y * 2 + (1 - c)
    cross = (1 - y) * 2 + c
    right = (g + 1) % groups
    left = (g + groups - 1) % groups

    def aligned(start):
        return pl.multiple_of(start, chunk)

    load_latents = pltpu.make_async_copy(latents_hbm, latents, local_sem.at[0])
    load_latents.start()
    parts = 3
    part_width = 3 * share // parts
    load_weight = [
        pltpu.make_async_copy(
            weight_hbm.at[:, pl.ds(part * part_width, part_width)],
            weight.at[:, pl.ds(part * part_width, part_width)],
            local_sem.at[1 + part],
        )
        for part in range(parts)
    ]
    for load in load_weight:
        load.start()
    load_out_weight = pltpu.make_async_copy(out_weight_hbm, out_weight, local_sem.at[4])
    load_cached = pltpu.make_async_copy(cached_hbm, attended, local_sem.at[5])

    barrier = pltpu.get_barrier_semaphore()
    for partner in ((g, sibling), (g, cross), (left, h), (right, h)):
        pl.semaphore_signal(barrier, inc=1, device_id=partner, device_id_type=MESH)
    pl.semaphore_wait(barrier, 4)

    load_latents.wait()
    to_sibling, to_cross = [], []
    for step in range(3):
        mine = (1 - y) * (2 - step) + y * step
        x = latents[pl.ds(aligned(mine * chunk), chunk), :].astype(F32)
        centred = x - jnp.mean(x, axis=-1, keepdims=True)
        variance = jnp.mean(centred * centred, axis=-1, keepdims=True)
        normed = (
            centred * lax.rsqrt(variance + 1e-06) * (1.0 + scale_ref[...]) + shift_ref[...]
        ).astype(BF16)
        place = aligned(c * rows + mine * chunk)
        near[pl.ds(place, chunk), :] = normed
        over = pltpu.make_async_remote_copy(
            src_ref=near.at[pl.ds(place, chunk), :],
            dst_ref=far.at[step, pl.ds(aligned(c * chunk), chunk), :],
            send_sem=cross_send.at[step],
            recv_sem=cross_recv.at[step],
            device_id=(g, cross),
            device_id_type=MESH,
        )
        over.start()
        to_cross.append(over)
        beside = pltpu.make_async_remote_copy(
            src_ref=near.at[pl.ds(place, chunk), :],
            dst_ref=near.at[pl.ds(place, chunk), :],
            send_sem=near_sib_send.at[step],
            recv_sem=near_sib_recv.at[step],
            device_id=(g, sibling),
            device_id_type=MESH,
        )
        beside.start()
        to_sibling.append(beside)

    def rim_tiles(reader, owner):
        used = [jnp.int32(0)] * 3
        for j in range(3):
            for w in range(window):
                entry = window_tiles_ref[reader, j, w]
                for t in range(3):
                    used[t] = used[t] | (entry == owner * 3 + t).astype(jnp.int32)
        spare = jnp.where(used[1] == 0, 1, jnp.where(used[0] == 0, 0, 2))
        return jnp.where(spare == 0, 1, 0), jnp.where(spare == 2, 1, 2)

    send_tiles = [rim_tiles(right, g), rim_tiles(left, g)]
    recv_tiles = [rim_tiles(g, left), rim_tiles(g, right)]
    candidates = [g * 3, g * 3 + 1, g * 3 + 2]
    for side, owner in ((0, left), (1, right)):
        candidates += [owner * 3 + recv_tiles[side][0], owner * 3 + recv_tiles[side][1]]
    named = []
    for j in range(3):
        hits = [jnp.int32(0)] * 7
        for w in range(window):
            entry = window_tiles_ref[g, j, w]
            inside = (w < window_count_ref[0, j]).astype(jnp.int32)
            for k in range(7):
                hits[k] = hits[k] + inside * (entry == candidates[k]).astype(jnp.int32)
        named.append(hits)
    for t in range(3):
        holds = [
            ((active_tiles_ref[0, j] == t) & (j < active_count_ref[0])).astype(jnp.int32)
            for j in range(3)
        ]
        for k in range(7):
            masks[t * 8 + k] = sum(holds[j] * named[j][k] for j in range(3)).astype(F32)
        masks[t * 8 + 7] = sum(holds).astype(F32)

    def head_norm(vectors, gain_ref):
        mean_square = jnp.mean(vectors * vectors, axis=-1, keepdims=True)
        return (vectors * lax.rsqrt(mean_square + 1e-06) * gain_ref[...]).astype(BF16)

    pair = 2 * 3 * HD

    def project(block, places):
        def body(step, carry):
            columns = pl.ds(pl.multiple_of(step * pair, pair), pair)
            packed = jnp.dot(block[...], weight[:, columns], preferred_element_type=F32)
            for half in range(2):
                at = half * 3 * HD
                head = step * 2 + half
                query_columns = pl.ds(pl.multiple_of(head * HD, HD), HD)
                value_columns = pl.ds(pl.multiple_of(share + head * HD, HD), HD)
                q = head_norm(packed[:, at : at + HD], query_gain_ref)
                k = head_norm(packed[:, at + HD : at + 2 * HD], key_gain_ref)
                v = packed[:, at + 2 * HD : at + 3 * HD].astype(BF16)
                for first, place, count in places:
                    queries[pl.ds(place, count), query_columns] = q[first : first + count]
                    bank[pl.ds(place, count), query_columns] = k[first : first + count]
                    bank[pl.ds(place, count), value_columns] = v[first : first + count]
            return carry

        lax.fori_loop(0, heads // 2, body, 0)

    order = ((0, 0), (0, 1), (0, 2), (1, 1), (0, 3), (1, 2), (1, 0), (1, 3))
    rim_copies = {}

    def send_rim(slot):
        second, quarter = order[slot]
        second = second + y * (1 - 2 * second)
        quarter = quarter + y * (3 - 2 * quarter)
        base = aligned((4 * second + quarter) * chunk)
        other = aligned((4 * second + quarter + 4) * chunk)
        low = bank[pl.ds(base, chunk), :]
        high = bank[pl.ds(other, chunk), :]
        for side in range(2):
            first_tile, second_tile = send_tiles[side]
            takes_high = jnp.where(second == 0, first_tile - 0, second_tile - 1)
            rim_send[side, slot] = jnp.where(takes_high == 1, high, low)
            copy = pltpu.make_async_remote_copy(
                src_ref=rim_send.at[side, slot],
                dst_ref=rim.at[side, second, pl.ds(aligned(quarter * chunk), chunk), :],
                send_sem=rim_send_sem.at[side, slot],
                recv_sem=rim_recv_sem.at[side, slot],
                device_id=(right if side == 0 else left, h),
                device_id_type=MESH,
            )
            copy.start()
            rim_copies[side, slot] = copy

    for load in load_weight:
        load.wait()
    load_out_weight.start()
    load_cached.start()
    for copy in to_sibling:
        copy.wait_recv()
    project(near, [(0, aligned(y * 2 * rows), 2 * rows)])
    send_rim(0)
    send_rim(1)
    passed = []
    for step in range(3):
        to_cross[step].wait_recv()
        onward = pltpu.make_async_remote_copy(
            src_ref=far.at[step, pl.ds(aligned(c * chunk), chunk), :],
            dst_ref=far.at[step, pl.ds(aligned(c * chunk), chunk), :],
            send_sem=pass_send.at[step],
            recv_sem=pass_recv.at[step],
            device_id=(g, sibling),
            device_id_type=MESH,
        )
        onward.start()
        passed.append(onward)
        onward.wait_recv()
        theirs = y * (2 - step) + (1 - y) * step
        start = (1 - y) * 2 * rows + theirs * chunk
        project(
            far.at[step],
            [(0, aligned(start), chunk), (chunk, aligned(start + rows), chunk)],
        )
        send_rim(2 * step + 2)
        send_rim(2 * step + 3)

    log_scale = math.log2(math.e) / math.sqrt(HD)

    def one_pair(q, k, v, mask):
        scores = lax.dot_general(q, k, (((1,), (1,)), ((), ())), preferred_element_type=F32)
        weights = jnp.exp2(scores * log_scale)
        folded = weights[:, :HD] if tile >= HD else jnp.pad(weights, ((0, 0), (0, HD - tile)))
        for at in range(HD, tile, HD):
            folded = folded + weights[:, at : at + HD]
        out = jnp.dot(weights.astype(BF16), v, preferred_element_type=F32)
        return out * mask, folded * mask

    def own_body(index, carry):
        t = index // heads
        head = index % heads
        here = pl.ds(aligned(t * tile), tile)
        columns = pl.ds(pl.multiple_of(head * HD, HD), HD)
        value_columns = pl.ds(pl.multiple_of(share + head * HD, HD), HD)
        q = queries[here, columns]
        out, total = None, None
        for k in range(3):
            there = pl.ds(k * tile, tile)
            more_out, more_total = one_pair(
                q, bank[there, columns], bank[there, value_columns], masks[t * 8 + k]
            )
            out = more_out if out is None else out + more_out
            total = more_total if total is None else total + more_total
        numerator[here, columns] = out
        totals[here, columns] = total
        return carry

    lax.fori_loop(0, 3 * heads, own_body, 0)

    def rim_sum(t, head, second):
        here = pl.ds(aligned(t * tile), tile)
        columns = pl.ds(pl.multiple_of(head * HD, HD), HD)
        value_columns = pl.ds(pl.multiple_of(share + head * HD, HD), HD)
        q = queries[here, columns]
        out, total = numerator[here, columns], totals[here, columns]
        for side in range(2):
            more_out, more_total = one_pair(
                q,
                rim[side, second, :, columns],
                rim[side, second, :, value_columns],
                masks[t * 8 + 3 + 2 * side + second],
            )
            out, total = out + more_out, total + more_total
        return here, columns, out, total

    def first_rim_body(index, carry):
        here, columns, out, total = rim_sum(index // heads, index % heads, y)
        numerator[here, columns] = out
        totals[here, columns] = total
        return carry

    def second_rim_tile(t):
        def body(head, carry):
            here, columns, out, total = rim_sum(t, head, 1 - y)
            slot_out = (out / jnp.sum(total, axis=-1, keepdims=True)).astype(BF16)
            attended[here, columns] = jnp.where(
                masks[t * 8 + 7] > 0.5, slot_out, attended[here, columns]
            )
            return carry

        lax.fori_loop(0, heads, body, 0)

    for slot in (0, 1, 2, 4):
        for side in range(2):
            rim_copies[side, slot].wait_recv()
    lax.fori_loop(0, 3 * heads, first_rim_body, 0)

    load_out_weight.wait()
    load_cached.wait()
    for copies in (to_sibling, to_cross, passed):
        for copy in copies:
            copy.wait_send()
    for slot in (3, 5, 6, 7):
        for side in range(2):
            rim_copies[side, slot].wait_recv()
    second_rim_tile((1 - y) * 2)
    second_rim_tile(1)

    def partial_sums(first, second):
        both = jnp.concatenate(
            [attended[pl.ds(aligned(first), chunk), :], attended[pl.ds(aligned(second), chunk), :]],
            axis=0,
        )
        return jnp.dot(both, out_weight[...], preferred_element_type=F32).astype(BF16)

    sums = []

    def project_out(slot, step, chip, chunk_at):
        owner = chip * 2 * rows + chunk_at * chunk
        both = partial_sums(owner + c * rows, owner + (1 - c) * rows)
        half = slot // 3
        near[pl.ds(half * rows + step * chunk, chunk), :] = both[:chunk]
        far[step, pl.ds(half * chunk, chunk), :] = both[chunk:]
        copy = pltpu.make_async_remote_copy(
            src_ref=far.at[step, pl.ds(half * chunk, chunk), :],
            dst_ref=sib_sums.at[slot],
            send_sem=sums_send.at[slot],
            recv_sem=sums_recv.at[slot],
            device_id=(g, sibling),
            device_id_type=MESH,
        )
        copy.start()
        sums.append(copy)

    last = []

    def send_last(step):
        sums[step].wait_recv()
        kept = near[pl.ds(step * chunk, chunk), :].astype(F32)
        near[pl.ds(step * chunk, chunk), :] = (kept + sib_sums[step].astype(F32)).astype(BF16)
        copy = pltpu.make_async_remote_copy(
            src_ref=near.at[pl.ds(step * chunk, chunk), :],
            dst_ref=cross_sums.at[step],
            send_sem=last_send.at[step],
            recv_sem=last_recv.at[step],
            device_id=(g, cross),
            device_id_type=MESH,
        )
        copy.start()
        last.append(copy)

    for step in range(3):
        project_out(step, step, 1 - y, step)
        if step > 0:
            send_last(step - 1)
    send_last(2)
    second_rim_tile(y * 2)
    for step in range(3):
        project_out(3 + step, step, y, step)
    stores = []
    for step in range(3):
        sums[3 + step].wait_recv()
        last[step].wait_recv()
        here = pl.ds(step * chunk, chunk)
        total = (
            near[pl.ds(rows + step * chunk, chunk), :].astype(F32)
            + sib_sums[3 + step].astype(F32)
            + cross_sums[step].astype(F32)
        )
        latents[here, :] = (latents[here, :].astype(F32) + gate_ref[...] * total).astype(BF16)
        store = pltpu.make_async_copy(
            latents.at[here, :], out_hbm.at[here, :], local_sem.at[step]
        )
        store.start()
        stores.append(store)
    for store in stores:
        store.wait()
    for copies in (sums, last, rim_copies.values()):
        for copy in copies:
            copy.wait_send()


def on_device(
    latents,
    mod_shift,
    mod_scale,
    mod_gate,
    packed_weight,
    query_gain,
    key_gain,
    output_weight,
    cached,
    active_tiles,
    active_count,
    window_tiles,
    window_count,
):
    rows, width = latents.shape
    groups, tiles, window = window_tiles.shape
    share = cached.shape[1]
    heads = share // HD
    slab = cached.shape[0]
    tile = slab // tiles
    chunk = tile // 4
    assert tiles == 3 and rows == 3 * chunk and slab == 4 * rows
    anywhere = pl.BlockSpec(memory_space=pl.ANY)
    vmem = pl.BlockSpec(memory_space=pltpu.VMEM)
    smem = pl.BlockSpec(memory_space=pltpu.SMEM)
    dma = pltpu.SemaphoreType.DMA
    return pl.pallas_call(
        functools.partial(kernel, (groups, heads, tile, width, window)),
        out_shape=jax.ShapeDtypeStruct((rows, width), BF16),
        in_specs=[
            anywhere,
            vmem,
            vmem,
            vmem,
            anywhere,
            vmem,
            vmem,
            anywhere,
            anywhere,
            smem,
            smem,
            smem,
            smem,
        ],
        out_specs=anywhere,
        scratch_shapes=[
            pltpu.VMEM((rows, width), BF16),
            pltpu.VMEM((2 * rows, width), BF16),
            pltpu.VMEM((3, 2 * chunk, width), BF16),
            pltpu.VMEM((width, 3 * share), BF16),
            pltpu.VMEM((slab, share), BF16),
            pltpu.VMEM((slab, 2 * share), BF16),
            pltpu.VMEM((2, 8, chunk, 2 * share), BF16),
            pltpu.VMEM((2, 2, tile, 2 * share), BF16),
            pltpu.VMEM((slab, share), F32),
            pltpu.VMEM((slab, share), F32),
            pltpu.VMEM((slab, share), BF16),
            pltpu.VMEM((share, width), BF16),
            pltpu.VMEM((6, chunk, width), BF16),
            pltpu.VMEM((3, chunk, width), BF16),
            pltpu.SMEM((24,), F32),
            dma((6,)),
            dma((3,)),
            dma((3,)),
            dma((3,)),
            dma((3,)),
            dma((3,)),
            dma((3,)),
            dma((2, 8)),
            dma((2, 8)),
            dma((6,)),
            dma((6,)),
            dma((3,)),
            dma((3,)),
        ],
        compiler_params=pltpu.CompilerParams(
            collective_id=0, has_side_effects=True, vmem_limit_bytes=VMEM_LIMIT
        ),
    )(
        latents,
        mod_shift[None],
        mod_scale[None],
        mod_gate[None],
        packed_weight,
        query_gain[None],
        key_gain[None],
        output_weight,
        cached,
        active_tiles,
        active_count,
        window_tiles,
        window_count,
    )


VMEM_LIMIT = 64 * 1024 * 1024


def solution(mesh):
    in_specs = (
        P(("frame", "head"), None),
        P(),
        P(),
        P(),
        P(None, "head"),
        P(),
        P(),
        P("head", None),
        P("frame", "head"),
        P("frame", None),
        P("frame"),
        P(),
        P("frame", None),
    )
    return jax.shard_map(
        on_device,
        mesh=mesh,
        in_specs=in_specs,
        out_specs=P(("frame", "head"), None),
        check_vma=False,
    )
```

time: 458 us -> 190 us (0.41)
  the two profiles are of different devices: /device:TPU:104 before, /device:TPU:0 now
where the time goes in v1:
time: 190 us
  Pallas kernels  185 us (97%)
  local copies, waits for them, and re-layouts  4.23 us (2%)
    pallas_call x1, Pallas kernels, on_device(): pl.pallas_call(functools.partial(kernel, (groups, heads, tile, width, win...  185 us
    unnamed x2, local copies, waits for them, and re-layouts  4.23 us

profile of v1, /device:TPU:0, one launch (start us, length us, event | category | flops | bytes accessed | tf_op | source)
XLA Modules:
  0.0 189.9 jit_solution(14299249754630177887)
XLA Ops:
  0.7 1.4 copy.14.window_tiles_ref
  2.1 185.0 %shard_map.127 = bf16[288,3072]{1,0:T(8,128)(2,1)} custom-call(bf16[288,3072]{1,0:T(8,128)(2,1)} %latents_hbm.1, f32[1,3072]{1,0:T(1,128)} %bitcast.5, f32[1,3072]{1,0:T(1,128)} %bitcast.6, f32[1,3072]{1,0:T(1,128)} %bitcast.7, bf16[3072,2304]{1,0:T(8,128)(2,1)} %weight_hbm.1, f32[1,128]{1,0:T(1,128)} %bitcast.8, f32[1,128]{1,0:T(1,128)} %bitcast.9, ...), custom_call_target="tpu_custom_call" | custom-call | tf_op jit(solution)/shard_map/pallas_call | solution.py:432
  187.1 2.8 %copy.17 = bf16[288,3072]{1,0:T(8,128)(2,1)} copy(bf16[288,3072]{1,0:T(8,128)(2,1)} %shard_map.127) | data formatting | bytes 3538944

commit v2 on v1

--- a/solution.py
+++ b/solution.py
@@ -9,6 +9,7 @@
 from jax.sharding import PartitionSpec as P
 
 HD = 128
+ROW = 4
 BF16 = jnp.bfloat16
 F32 = jnp.float32
 MESH = pl.DeviceIdType.MESH
@@ -31,18 +32,17 @@
     window_count_ref,
     out_hbm,
     latents,
-    near,
-    far,
+    rows_buffer,
     weight,
     queries,
     bank,
     rim_send,
     rim,
+    rim_rows,
     numerator,
     totals,
     attended,
     out_weight,
-    sib_sums,
     cross_sums,
     masks,
     local_sem,
@@ -54,10 +54,13 @@
     pass_recv,
     rim_send_sem,
     rim_recv_sem,
+    rim_pass_send,
+    rim_pass_recv,
     sums_send,
     sums_recv,
     last_send,
     last_recv,
+    free_sem,
 ):
     groups, heads, tile, width, window = sizes
     share = heads * HD
@@ -71,9 +74,17 @@
     cross = (1 - y) * 2 + c
     right = (g + 1) % groups
     left = (g + groups - 1) % groups
+    left_edge = (ROW - g % ROW) // ROW
+    right_edge = (g % ROW + 1) // ROW
+    left_partner = (left, h + left_edge * (cross - h))
+    right_partner = (right, h + right_edge * (cross - h))
+    edge_side = right_edge
 
     def aligned(start):
         return pl.multiple_of(start, chunk)
+
+    def far_place(step, core):
+        return aligned((6 + 2 * step + core) * chunk)
 
     load_latents = pltpu.make_async_copy(latents_hbm, latents, local_sem.at[0])
     load_latents.start()
@@ -93,7 +104,7 @@
     load_cached = pltpu.make_async_copy(cached_hbm, attended, local_sem.at[5])
 
     barrier = pltpu.get_barrier_semaphore()
-    for partner in ((g, sibling), (g, cross), (left, h), (right, h)):
+    for partner in ((g, sibling), (g, cross), left_partner, right_partner):
         pl.semaphore_signal(barrier, inc=1, device_id=partner, device_id_type=MESH)
     pl.semaphore_wait(barrier, 4)
 
@@ -108,10 +119,10 @@
             centred * lax.rsqrt(variance + 1e-06) * (1.0 + scale_ref[...]) + shift_ref[...]
         ).astype(BF16)
         place = aligned(c * rows + mine * chunk)
-        near[pl.ds(place, chunk), :] = normed
+        rows_buffer[pl.ds(place, chunk), :] = normed
         over = pltpu.make_async_remote_copy(
-            src_ref=near.at[pl.ds(place, chunk), :],
-            dst_ref=far.at[step, pl.ds(aligned(c * chunk), chunk), :],
+            src_ref=rows_buffer.at[pl.ds(place, chunk), :],
+            dst_ref=rows_buffer.at[pl.ds(far_place(step, c), chunk), :],
             send_sem=cross_send.at[step],
             recv_sem=cross_recv.at[step],
             device_id=(g, cross),
@@ -120,8 +131,8 @@
         over.start()
         to_cross.append(over)
         beside = pltpu.make_async_remote_copy(
-            src_ref=near.at[pl.ds(place, chunk), :],
-            dst_ref=near.at[pl.ds(place, chunk), :],
+            src_ref=rows_buffer.at[pl.ds(place, chunk), :],
+            dst_ref=rows_buffer.at[pl.ds(place, chunk), :],
             send_sem=near_sib_send.at[step],
             recv_sem=near_sib_recv.at[step],
             device_id=(g, sibling),
@@ -169,10 +180,10 @@
 
     pair = 2 * 3 * HD
 
-    def project(block, places):
+    def project(block_at, places):
         def body(step, carry):
             columns = pl.ds(pl.multiple_of(step * pair, pair), pair)
-            packed = jnp.dot(block[...], weight[:, columns], preferred_element_type=F32)
+            packed = jnp.dot(rows_buffer[block_at, :], weight[:, columns], preferred_element_type=F32)
             for half in range(2):
                 at = half * 3 * HD
                 head = step * 2 + half
@@ -190,30 +201,171 @@
         lax.fori_loop(0, heads // 2, body, 0)
 
     order = ((0, 0), (0, 1), (0, 2), (1, 1), (0, 3), (1, 2), (1, 0), (1, 3))
-    rim_copies = {}
-
-    def send_rim(slot):
+
+    def quarter_of(slot, chip):
         second, quarter = order[slot]
-        second = second + y * (1 - 2 * second)
-        quarter = quarter + y * (3 - 2 * quarter)
-        base = aligned((4 * second + quarter) * chunk)
-        other = aligned((4 * second + quarter + 4) * chunk)
-        low = bank[pl.ds(base, chunk), :]
-        high = bank[pl.ds(other, chunk), :]
+        return second + chip * (1 - 2 * second), quarter + chip * (3 - 2 * quarter)
+
+    def row_place(piece):
+        chip, inside = piece // 6, piece % 6
+        away = (chip + y) % 2
+        number = inside % 3
+        step = y * (2 - number) + (1 - y) * number
+        return aligned(
+            (1 - away) * inside * chunk + away * (6 + 2 * step + inside // 3) * chunk
+        )
+
+    half_width = width // 2
+
+    def tile_copy(side, slot):
+        second, quarter = quarter_of(slot, y)
+        return pltpu.make_async_remote_copy(
+            src_ref=rim_send.at[side, slot],
+            dst_ref=rim.at[side, second, pl.ds(aligned(quarter * chunk), chunk), :],
+            send_sem=rim_send_sem.at[side, slot],
+            recv_sem=rim_recv_sem.at[side, slot],
+            device_id=(right if side == 0 else left, h),
+            device_id_type=MESH,
+        )
+
+    def edge_copy(side, slot):
+        stage, half = slot // 2, slot % 2
+        target = left + (1 - side) * (right - left)
+        return pltpu.make_async_remote_copy(
+            src_ref=rim_send.at[side, slot],
+            dst_ref=rim_rows.at[
+                pl.ds(aligned((2 * stage + c) * chunk), chunk),
+                pl.ds(half * half_width, half_width),
+            ],
+            send_sem=rim_send_sem.at[side, slot],
+            recv_sem=rim_recv_sem.at[side, slot],
+            device_id=(target, cross),
+            device_id_type=MESH,
+        )
+
+    def edge_pass(stage):
+        here = pl.ds(aligned((2 * stage + c) * chunk), chunk)
+        return pltpu.make_async_remote_copy(
+            src_ref=rim_rows.at[here, :],
+            dst_ref=rim_rows.at[here, :],
+            send_sem=rim_pass_send.at[stage],
+            recv_sem=rim_pass_recv.at[stage],
+            device_id=(g, sibling),
+            device_id_type=MESH,
+        )
+
+    def takes_high(side, second):
+        first_tile, second_tile = send_tiles[side]
+        return jnp.where(second == 0, first_tile, second_tile - 1) == 1
+
+    def send_rim(stage):
         for side in range(2):
-            first_tile, second_tile = send_tiles[side]
-            takes_high = jnp.where(second == 0, first_tile - 0, second_tile - 1)
-            rim_send[side, slot] = jnp.where(takes_high == 1, high, low)
-            copy = pltpu.make_async_remote_copy(
-                src_ref=rim_send.at[side, slot],
-                dst_ref=rim.at[side, second, pl.ds(aligned(quarter * chunk), chunk), :],
-                send_sem=rim_send_sem.at[side, slot],
-                recv_sem=rim_recv_sem.at[side, slot],
-                device_id=(right if side == 0 else left, h),
-                device_id_type=MESH,
+            edge = right_edge if side == 0 else left_edge
+
+            @pl.when(edge == 0)
+            def _():
+                for slot in (2 * stage, 2 * stage + 1):
+                    second, quarter = quarter_of(slot, y)
+                    low = bank[pl.ds(aligned((4 * second + quarter) * chunk), chunk), :]
+                    high = bank[pl.ds(aligned((4 * second + quarter + 4) * chunk), chunk), :]
+                    rim_send[side, slot] = jnp.where(takes_high(side, second), high, low)
+                    tile_copy(side, slot).start()
+
+            @pl.when(edge == 1)
+            def _():
+                second, quarter = (
+                    (1 - c) * even + c * odd
+                    for even, odd in zip(quarter_of(2 * stage, y), quarter_of(2 * stage + 1, y))
+                )
+                low = row_place(4 * second + quarter)
+                high = row_place(4 * second + quarter + 4)
+                for half in range(2):
+                    columns = pl.ds(half * half_width, half_width)
+                    rim_send[side, 2 * stage + half] = jnp.where(
+                        takes_high(side, second),
+                        rows_buffer[pl.ds(high, chunk), columns],
+                        rows_buffer[pl.ds(low, chunk), columns],
+                    )
+                    edge_copy(side, 2 * stage + half).start()
+
+    def wait_rim(slots):
+        for side in range(2):
+            edge = left_edge if side == 0 else right_edge
+
+            @pl.when(edge == 0)
+            def _():
+                for slot in slots:
+                    tile_copy(side, slot).wait_recv()
+
+    def edge_stages(stages):
+        @pl.when(left_edge + right_edge == 1)
+        def _():
+            for stage in stages:
+                for half in range(2):
+                    edge_copy(edge_side, 2 * stage + half).wait_recv()
+                edge_pass(stage).start()
+            for stage in stages:
+                edge_pass(stage).wait_recv()
+                places = []
+                for core in range(2):
+                    second, quarter = quarter_of(2 * stage + core, 1 - y)
+                    places.append((core * chunk, second, aligned(quarter * chunk)))
+
+                def body(head, carry):
+                    columns = pl.ds(pl.multiple_of(head * 3 * HD + HD, HD), 2 * HD)
+                    packed = jnp.dot(
+                        rim_rows[pl.ds(2 * stage * chunk, 2 * chunk), :],
+                        weight[:, columns],
+                        preferred_element_type=F32,
+                    )
+                    k = head_norm(packed[:, :HD], key_gain_ref)
+                    v = packed[:, HD:].astype(BF16)
+                    key_columns = pl.ds(pl.multiple_of(head * HD, HD), HD)
+                    value_columns = pl.ds(pl.multiple_of(share + head * HD, HD), HD)
+                    for first, second, place in places:
+                        there = pl.ds(place, chunk)
+                        rim[edge_side, second, there, key_columns] = k[first : first + chunk]
+                        rim[edge_side, second, there, value_columns] = v[first : first + chunk]
+                    return carry
+
+                lax.fori_loop(0, heads, body, 0)
+
+    log_scale = math.log2(math.e) / math.sqrt(HD)
+    near_tile = y * 2
+    far_tile = (1 - y) * 2
+
+    def attend(q, keys, values, names):
+        result = None
+        for k, v, name in zip(keys, values, names):
+            scores = lax.dot_general(
+                q, k, (((1,), (1,)), ((), ())), preferred_element_type=F32
             )
-            copy.start()
-            rim_copies[side, slot] = copy
+            weights = jnp.exp2(scores * log_scale).astype(BF16)
+            both = jnp.concatenate([v, jnp.ones_like(v)], axis=1)
+            both = jnp.where(name > 0.5, both, jnp.zeros_like(both))
+            out = jnp.dot(weights, both, preferred_element_type=F32)
+            result = out if result is None else result + out
+        return result[:, :HD], result[:, HD:]
+
+    def own_pairs(t, others, first):
+        def body(head, carry):
+            here = pl.ds(aligned(t * tile), tile)
+            columns = pl.ds(pl.multiple_of(head * HD, HD), HD)
+            value_columns = pl.ds(pl.multiple_of(share + head * HD, HD), HD)
+            there = [pl.ds(aligned(other * tile), tile) for other in others]
+            out, total = attend(
+                queries[here, columns],
+                [bank[place, columns] for place in there],
+                [bank[place, value_columns] for place in there],
+                [masks[t * 8 + other] for other in others],
+            )
+            if not first:
+                out, total = numerator[here, columns] + out, totals[here, columns] + total
+            numerator[here, columns] = out
+            totals[here, columns] = total
+            return carry
+
+        lax.fori_loop(0, heads, body, 0)
 
     for load in load_weight:
         load.wait()
@@ -221,15 +373,14 @@
     load_cached.start()
     for copy in to_sibling:
         copy.wait_recv()
-    project(near, [(0, aligned(y * 2 * rows), 2 * rows)])
+    project(pl.ds(0, 2 * rows), [(0, aligned(y * 2 * rows), 2 * rows)])
     send_rim(0)
-    send_rim(1)
     passed = []
     for step in range(3):
         to_cross[step].wait_recv()
         onward = pltpu.make_async_remote_copy(
-            src_ref=far.at[step, pl.ds(aligned(c * chunk), chunk), :],
-            dst_ref=far.at[step, pl.ds(aligned(c * chunk), chunk), :],
+            src_ref=rows_buffer.at[pl.ds(far_place(step, c), chunk), :],
+            dst_ref=rows_buffer.at[pl.ds(far_place(step, c), chunk), :],
             send_sem=pass_send.at[step],
             recv_sem=pass_recv.at[step],
             device_id=(g, sibling),
@@ -241,70 +392,43 @@
         theirs = y * (2 - step) + (1 - y) * step
         start = (1 - y) * 2 * rows + theirs * chunk
         project(
-            far.at[step],
+            pl.ds(far_place(step, 0), 2 * chunk),
             [(0, aligned(start), chunk), (chunk, aligned(start + rows), chunk)],
         )
-        send_rim(2 * step + 2)
-        send_rim(2 * step + 3)
-
-    log_scale = math.log2(math.e) / math.sqrt(HD)
-
-    def one_pair(q, k, v, mask):
-        scores = lax.dot_general(q, k, (((1,), (1,)), ((), ())), preferred_element_type=F32)
-        weights = jnp.exp2(scores * log_scale)
-        folded = weights[:, :HD] if tile >= HD else jnp.pad(weights, ((0, 0), (0, HD - tile)))
-        for at in range(HD, tile, HD):
-            folded = folded + weights[:, at : at + HD]
-        out = jnp.dot(weights.astype(BF16), v, preferred_element_type=F32)
-        return out * mask, folded * mask
-
-    def own_body(index, carry):
-        t = index // heads
-        head = index % heads
+        send_rim(step + 1)
+        if step == 0:
+            own_pairs(near_tile, [near_tile], True)
+        if step == 1:
+            own_pairs(near_tile, [1], False)
+            own_pairs(1, [near_tile, 1], True)
+    own_pairs(near_tile, [far_tile], False)
+    own_pairs(1, [far_tile], False)
+    own_pairs(far_tile, [near_tile, 1, far_tile], True)
+
+    def rim_sum(t, head, phase):
         here = pl.ds(aligned(t * tile), tile)
         columns = pl.ds(pl.multiple_of(head * HD, HD), HD)
         value_columns = pl.ds(pl.multiple_of(share + head * HD, HD), HD)
-        q = queries[here, columns]
-        out, total = None, None
-        for k in range(3):
-            there = pl.ds(k * tile, tile)
-            more_out, more_total = one_pair(
-                q, bank[there, columns], bank[there, value_columns], masks[t * 8 + k]
-            )
-            out = more_out if out is None else out + more_out
-            total = more_total if total is None else total + more_total
+        keys, values, names = [], [], []
+        for side in range(2):
+            edge = left_edge if side == 0 else right_edge
+            second = (y + edge + phase) % 2
+            keys.append(rim[side, second, :, columns])
+            values.append(rim[side, second, :, value_columns])
+            names.append(masks[t * 8 + 3 + 2 * side + second])
+        out, total = attend(queries[here, columns], keys, values, names)
+        return here, columns, numerator[here, columns] + out, totals[here, columns] + total
+
+    def first_rim_body(index, carry):
+        here, columns, out, total = rim_sum(index // heads, index % heads, 0)
         numerator[here, columns] = out
         totals[here, columns] = total
         return carry
 
-    lax.fori_loop(0, 3 * heads, own_body, 0)
-
-    def rim_sum(t, head, second):
-        here = pl.ds(aligned(t * tile), tile)
-        columns = pl.ds(pl.multiple_of(head * HD, HD), HD)
-        value_columns = pl.ds(pl.multiple_of(share + head * HD, HD), HD)
-        q = queries[here, columns]
-        out, total = numerator[here, columns], totals[here, columns]
-        for side in range(2):
-            more_out, more_total = one_pair(
-                q,
-                rim[side, second, :, columns],
-                rim[side, second, :, value_columns],
-                masks[t * 8 + 3 + 2 * side + second],
-            )
-            out, total = out + more_out, total + more_total
-        return here, columns, out, total
-
-    def first_rim_body(index, carry):
-        here, columns, out, total = rim_sum(index // heads, index % heads, y)
-        numerator[here, columns] = out
-        totals[here, columns] = total
-        return carry
-
     def second_rim_tile(t):
         def body(head, carry):
-            here, columns, out, total = rim_sum(t, head, 1 - y)
-            slot_out = (out / jnp.sum(total, axis=-1, keepdims=True)).astype(BF16)
+            here, columns, out, total = rim_sum(t, head, 1)
+            slot_out = (out / total).astype(BF16)
             attended[here, columns] = jnp.where(
                 masks[t * 8 + 7] > 0.5, slot_out, attended[here, columns]
             )
@@ -312,9 +436,8 @@
 
         lax.fori_loop(0, heads, body, 0)
 
-    for slot in (0, 1, 2, 4):
-        for side in range(2):
-            rim_copies[side, slot].wait_recv()
+    wait_rim((0, 1, 2, 4))
+    edge_stages((0, 1, 2))
     lax.fori_loop(0, 3 * heads, first_rim_body, 0)
 
     load_out_weight.wait()
@@ -322,11 +445,18 @@
     for copies in (to_sibling, to_cross, passed):
         for copy in copies:
             copy.wait_send()
-    for slot in (3, 5, 6, 7):
-        for side in range(2):
-            rim_copies[side, slot].wait_recv()
-    second_rim_tile((1 - y) * 2)
+    wait_rim((3, 5, 6, 7))
+    edge_stages((3,))
+
+    @pl.when(left_edge + right_edge == 1)
+    def _():
+        for stage in range(4):
+            edge_pass(stage).wait_send()
+
+    pl.semaphore_signal(free_sem, inc=1, device_id=(g, sibling), device_id_type=MESH)
+    second_rim_tile(far_tile)
     second_rim_tile(1)
+    pl.semaphore_wait(free_sem, 1)
 
     def partial_sums(first, second):
         both = jnp.concatenate(
@@ -341,11 +471,11 @@
         owner = chip * 2 * rows + chunk_at * chunk
         both = partial_sums(owner + c * rows, owner + (1 - c) * rows)
         half = slot // 3
-        near[pl.ds(half * rows + step * chunk, chunk), :] = both[:chunk]
-        far[step, pl.ds(half * chunk, chunk), :] = both[chunk:]
+        rows_buffer[pl.ds((3 * half + step) * chunk, chunk), :] = both[:chunk]
+        rows_buffer[pl.ds((6 + slot) * chunk, chunk), :] = both[chunk:]
         copy = pltpu.make_async_remote_copy(
-            src_ref=far.at[step, pl.ds(half * chunk, chunk), :],
-            dst_ref=sib_sums.at[slot],
+            src_ref=rows_buffer.at[pl.ds((6 + slot) * chunk, chunk), :],
+            dst_ref=rim_rows.at[pl.ds(slot * chunk, chunk), :],
             send_sem=sums_send.at[slot],
             recv_sem=sums_recv.at[slot],
             device_id=(g, sibling),
@@ -358,10 +488,11 @@
 
     def send_last(step):
         sums[step].wait_recv()
-        kept = near[pl.ds(step * chunk, chunk), :].astype(F32)
-        near[pl.ds(step * chunk, chunk), :] = (kept + sib_sums[step].astype(F32)).astype(BF16)
+        here = pl.ds(step * chunk, chunk)
+        kept = rows_buffer[here, :].astype(F32)
+        rows_buffer[here, :] = (kept + rim_rows[here, :].astype(F32)).astype(BF16)
         copy = pltpu.make_async_remote_copy(
-            src_ref=near.at[pl.ds(step * chunk, chunk), :],
+            src_ref=rows_buffer.at[pl.ds(step * chunk, chunk), :],
             dst_ref=cross_sums.at[step],
             send_sem=last_send.at[step],
             recv_sem=last_recv.at[step],
@@ -376,7 +507,7 @@
         if step > 0:
             send_last(step - 1)
     send_last(2)
-    second_rim_tile(y * 2)
+    second_rim_tile(near_tile)
     for step in range(3):
         project_out(3 + step, step, y, step)
     stores = []
@@ -385,8 +516,8 @@
         last[step].wait_recv()
         here = pl.ds(step * chunk, chunk)
         total = (
-            near[pl.ds(rows + step * chunk, chunk), :].astype(F32)
-            + sib_sums[3 + step].astype(F32)
+            rows_buffer[pl.ds((3 + step) * chunk, chunk), :].astype(F32)
+            + rim_rows[pl.ds((3 + step) * chunk, chunk), :].astype(F32)
             + cross_sums[step].astype(F32)
         )
         latents[here, :] = (latents[here, :].astype(F32) + gate_ref[...] * total).astype(BF16)
@@ -397,9 +528,11 @@
         stores.append(store)
     for store in stores:
         store.wait()
-    for copies in (sums, last, rim_copies.values()):
-        for copy in copies:
-            copy.wait_send()
+    for copy in sums + last:
+        copy.wait_send()
+    for side in range(2):
+        for slot in range(8):
+            tile_copy(side, slot).wait_send()
 
 
 def on_device(
@@ -424,7 +557,7 @@
     slab = cached.shape[0]
     tile = slab // tiles
     chunk = tile // 4
-    assert tiles == 3 and rows == 3 * chunk and slab == 4 * rows
+    assert width == 4 * share and tiles == 3 and rows == 3 * chunk and slab == 4 * rows
     anywhere = pl.BlockSpec(memory_space=pl.ANY)
     vmem = pl.BlockSpec(memory_space=pltpu.VMEM)
     smem = pl.BlockSpec(memory_space=pltpu.SMEM)
@@ -450,18 +583,17 @@
         out_specs=anywhere,
         scratch_shapes=[
             pltpu.VMEM((rows, width), BF16),
-            pltpu.VMEM((2 * rows, width), BF16),
-            pltpu.VMEM((3, 2 * chunk, width), BF16),
+            pltpu.VMEM((slab, width), BF16),
             pltpu.VMEM((width, 3 * share), BF16),
             pltpu.VMEM((slab, share), BF16),
             pltpu.VMEM((slab, 2 * share), BF16),
             pltpu.VMEM((2, 8, chunk, 2 * share), BF16),
             pltpu.VMEM((2, 2, tile, 2 * share), BF16),
+            pltpu.VMEM((8 * chunk, width), BF16),
             pltpu.VMEM((slab, share), F32),
             pltpu.VMEM((slab, share), F32),
             pltpu.VMEM((slab, share), BF16),
             pltpu.VMEM((share, width), BF16),
-            pltpu.VMEM((6, chunk, width), BF16),
             pltpu.VMEM((3, chunk, width), BF16),
             pltpu.SMEM((24,), F32),
             dma((6,)),
@@ -473,10 +605,13 @@
             dma((3,)),
             dma((2, 8)),
             dma((2, 8)),
+            dma((4,)),
+            dma((4,)),
             dma((6,)),
             dma((6,)),
             dma((3,)),
             dma((3,)),
+            pltpu.SemaphoreType.REGULAR,
         ],
         compiler_params=pltpu.CompilerParams(
             collective_id=0, has_side_effects=True, vmem_limit_bytes=VMEM_LIMIT

time: 190 us -> 155 us (0.82)
  the two profiles are of different devices: /device:TPU:0 before, /device:TPU:1 now
where the time goes in v2:
time: 155 us
  Pallas kernels  150 us (97%)
  local copies, waits for them, and re-layouts  4.23 us (3%)
    pallas_call x1, Pallas kernels, on_device(): pl.pallas_call(functools.partial(kernel, (groups, heads, tile, width, win...  150 us
    unnamed x2, local copies, waits for them, and re-layouts  4.23 us

profile of v2, /device:TPU:1, one launch (start us, length us, event | category | flops | bytes accessed | tf_op | source)
XLA Modules:
  0.0 154.7 jit_solution(7439116733962194619)
XLA Ops:
  0.7 1.4 copy.14.window_tiles_ref
  2.1 149.8 %shard_map.127 = bf16[288,3072]{1,0:T(8,128)(2,1)} custom-call(bf16[288,3072]{1,0:T(8,128)(2,1)} %latents_hbm.1, f32[1,3072]{1,0:T(1,128)} %bitcast.5, f32[1,3072]{1,0:T(1,128)} %bitcast.6, f32[1,3072]{1,0:T(1,128)} %bitcast.7, bf16[3072,2304]{1,0:T(8,128)(2,1)} %weight_hbm.1, f32[1,128]{1,0:T(1,128)} %bitcast.8, f32[1,128]{1,0:T(1,128)} %bitcast.9, ...), custom_call_target="tpu_custom_call" | custom-call | tf_op jit(solution)/shard_map/pallas_call | solution.py:565
  151.9 2.8 %copy.17 = bf16[288,3072]{1,0:T(8,128)(2,1)} copy(bf16[288,3072]{1,0:T(8,128)(2,1)} %shard_map.127) | data formatting | bytes 3538944

commit v3 on v2

--- a/solution.py
+++ b/solution.py
@@ -258,7 +258,7 @@
         first_tile, second_tile = send_tiles[side]
         return jnp.where(second == 0, first_tile, second_tile - 1) == 1
 
-    def send_rim(stage):
+    def send_tiles_of(stage):
         for side in range(2):
             edge = right_edge if side == 0 else left_edge
 
@@ -270,6 +270,10 @@
                     high = bank[pl.ds(aligned((4 * second + quarter + 4) * chunk), chunk), :]
                     rim_send[side, slot] = jnp.where(takes_high(side, second), high, low)
                     tile_copy(side, slot).start()
+
+    def send_rows_of(stage):
+        for side in range(2):
+            edge = right_edge if side == 0 else left_edge
 
             @pl.when(edge == 1)
             def _():
@@ -297,21 +301,24 @@
                 for slot in slots:
                     tile_copy(side, slot).wait_recv()
 
-    def edge_stages(stages):
+    def pass_edge(stage):
         @pl.when(left_edge + right_edge == 1)
         def _():
-            for stage in stages:
-                for half in range(2):
-                    edge_copy(edge_side, 2 * stage + half).wait_recv()
-                edge_pass(stage).start()
-            for stage in stages:
-                edge_pass(stage).wait_recv()
-                places = []
-                for core in range(2):
-                    second, quarter = quarter_of(2 * stage + core, 1 - y)
-                    places.append((core * chunk, second, aligned(quarter * chunk)))
-
-                def body(head, carry):
+            for half in range(2):
+                edge_copy(edge_side, 2 * stage + half).wait_recv()
+            edge_pass(stage).start()
+
+    def project_edge(stage):
+        @pl.when(left_edge + right_edge == 1)
+        def _():
+            edge_pass(stage).wait_recv()
+            places = []
+            for core in range(2):
+                second, quarter = quarter_of(2 * stage + core, 1 - y)
+                places.append((core * chunk, second, aligned(quarter * chunk)))
+
+            def body(step, carry):
+                for head in (2 * step, 2 * step + 1):
                     columns = pl.ds(pl.multiple_of(head * 3 * HD + HD, HD), 2 * HD)
                     packed = jnp.dot(
                         rim_rows[pl.ds(2 * stage * chunk, 2 * chunk), :],
@@ -326,46 +333,81 @@
                         there = pl.ds(place, chunk)
                         rim[edge_side, second, there, key_columns] = k[first : first + chunk]
                         rim[edge_side, second, there, value_columns] = v[first : first + chunk]
-                    return carry
-
-                lax.fori_loop(0, heads, body, 0)
+                return carry
+
+            lax.fori_loop(0, heads // 2, body, 0)
 
     log_scale = math.log2(math.e) / math.sqrt(HD)
     near_tile = y * 2
     far_tile = (1 - y) * 2
 
     def attend(q, keys, values, names):
-        result = None
-        for k, v, name in zip(keys, values, names):
-            scores = lax.dot_general(
-                q, k, (((1,), (1,)), ((), ())), preferred_element_type=F32
-            )
-            weights = jnp.exp2(scores * log_scale).astype(BF16)
-            both = jnp.concatenate([v, jnp.ones_like(v)], axis=1)
-            both = jnp.where(name > 0.5, both, jnp.zeros_like(both))
-            out = jnp.dot(weights, both, preferred_element_type=F32)
-            result = out if result is None else result + out
-        return result[:, :HD], result[:, HD:]
-
-    def own_pairs(t, others, first):
-        def body(head, carry):
-            here = pl.ds(aligned(t * tile), tile)
-            columns = pl.ds(pl.multiple_of(head * HD, HD), HD)
-            value_columns = pl.ds(pl.multiple_of(share + head * HD, HD), HD)
-            there = [pl.ds(aligned(other * tile), tile) for other in others]
-            out, total = attend(
-                queries[here, columns],
-                [bank[place, columns] for place in there],
-                [bank[place, value_columns] for place in there],
-                [masks[t * 8 + other] for other in others],
-            )
-            if not first:
-                out, total = numerator[here, columns] + out, totals[here, columns] + total
+        scores = lax.dot_general(q, keys, (((1,), (1,)), ((), ())), preferred_element_type=F32)
+        weights = jnp.exp2(scores * log_scale)
+        weights = jnp.concatenate(
+            [weights[:, k * tile : (k + 1) * tile] * name for k, name in enumerate(names)], axis=1
+        )
+        total = weights[:, :HD]
+        for at in range(HD, weights.shape[1], HD):
+            total = total + weights[:, at : at + HD]
+        return jnp.dot(weights.astype(BF16), values, preferred_element_type=F32), total
+
+    def columns_of(head):
+        return (
+            pl.ds(pl.multiple_of(head * HD, HD), HD),
+            pl.ds(pl.multiple_of(share + head * HD, HD), HD),
+        )
+
+    def over_heads(work, unroll):
+        def body(step, carry):
+            for inner in range(unroll):
+                work(step * unroll + inner)
+            return carry
+
+        lax.fori_loop(0, heads // unroll, body, 0)
+
+    def own_pairs(t, first_key, count, fresh, head):
+        here = pl.ds(aligned(t * tile), tile)
+        there = pl.ds(aligned(first_key * tile), count * tile)
+        columns, value_columns = columns_of(head)
+        out, total = attend(
+            queries[here, columns],
+            bank[there, columns],
+            bank[there, value_columns],
+            [masks[t * 8 + first_key + k] for k in range(count)],
+        )
+        if not fresh:
+            out, total = numerator[here, columns] + out, totals[here, columns] + total
+        numerator[here, columns] = out
+        totals[here, columns] = total
+
+    def rim_pairs(t, phase, head):
+        here = pl.ds(aligned(t * tile), tile)
+        columns, value_columns = columns_of(head)
+        keys, values, names = [], [], []
+        for side in range(2):
+            edge = left_edge if side == 0 else right_edge
+            second = (y + edge + phase) % 2
+            keys.append(rim[side, second, :, columns])
+            values.append(rim[side, second, :, value_columns])
+            names.append(masks[t * 8 + 3 + 2 * side + second])
+        out, total = attend(
+            queries[here, columns],
+            jnp.concatenate(keys, axis=0),
+            jnp.concatenate(values, axis=0),
+            names,
+        )
+        out, total = numerator[here, columns] + out, totals[here, columns] + total
+        if phase == 0:
             numerator[here, columns] = out
             totals[here, columns] = total
-            return carry
-
-        lax.fori_loop(0, heads, body, 0)
+        else:
+            slot_out = (out / jnp.sum(total, axis=-1, keepdims=True)).astype(BF16)
+            attended[here, columns] = jnp.where(
+                masks[t * 8 + 7] > 0.5, slot_out, attended[here, columns]
+            )
+
+    half_heads = heads // 2
 
     for load in load_weight:
         load.wait()
@@ -373,8 +415,9 @@
     load_cached.start()
     for copy in to_sibling:
         copy.wait_recv()
+    send_rows_of(0)
     project(pl.ds(0, 2 * rows), [(0, aligned(y * 2 * rows), 2 * rows)])
-    send_rim(0)
+    send_tiles_of(0)
     passed = []
     for step in range(3):
         to_cross[step].wait_recv()
@@ -389,64 +432,51 @@
         onward.start()
         passed.append(onward)
         onward.wait_recv()
+        send_rows_of(step + 1)
+        if step > 0:
+            pass_edge(step - 1)
         theirs = y * (2 - step) + (1 - y) * step
         start = (1 - y) * 2 * rows + theirs * chunk
         project(
             pl.ds(far_place(step, 0), 2 * chunk),
             [(0, aligned(start), chunk), (chunk, aligned(start + rows), chunk)],
         )
-        send_rim(step + 1)
+        send_tiles_of(step + 1)
         if step == 0:
-            own_pairs(near_tile, [near_tile], True)
+            over_heads(lambda head: own_pairs(near_tile, near_tile, 1, True, head), half_heads)
         if step == 1:
-            own_pairs(near_tile, [1], False)
-            own_pairs(1, [near_tile, 1], True)
-    own_pairs(near_tile, [far_tile], False)
-    own_pairs(1, [far_tile], False)
-    own_pairs(far_tile, [near_tile, 1, far_tile], True)
-
-    def rim_sum(t, head, phase):
-        here = pl.ds(aligned(t * tile), tile)
-        columns = pl.ds(pl.multiple_of(head * HD, HD), HD)
-        value_columns = pl.ds(pl.multiple_of(share + head * HD, HD), HD)
-        keys, values, names = [], [], []
-        for side in range(2):
-            edge = left_edge if side == 0 else right_edge
-            second = (y + edge + phase) % 2
-            keys.append(rim[side, second, :, columns])
-            values.append(rim[side, second, :, value_columns])
-            names.append(masks[t * 8 + 3 + 2 * side + second])
-        out, total = attend(queries[here, columns], keys, values, names)
-        return here, columns, numerator[here, columns] + out, totals[here, columns] + total
-
-    def first_rim_body(index, carry):
-        here, columns, out, total = rim_sum(index // heads, index % heads, 0)
-        numerator[here, columns] = out
-        totals[here, columns] = total
-        return carry
-
-    def second_rim_tile(t):
-        def body(head, carry):
-            here, columns, out, total = rim_sum(t, head, 1)
-            slot_out = (out / total).astype(BF16)
-            attended[here, columns] = jnp.where(
-                masks[t * 8 + 7] > 0.5, slot_out, attended[here, columns]
-            )
-            return carry
-
-        lax.fori_loop(0, heads, body, 0)
-
+
+            def two_tiles(head):
+                own_pairs(near_tile, 1, 1, False, head)
+                own_pairs(1, y, 2, True, head)
+
+            over_heads(two_tiles, 1)
+            project_edge(0)
+    project_edge(1)
+    pass_edge(2)
+
+    def three_tiles(head):
+        own_pairs(near_tile, far_tile, 1, False, head)
+        own_pairs(1, far_tile, 1, False, head)
+        own_pairs(far_tile, 0, 3, True, head)
+
+    over_heads(three_tiles, 1)
+    project_edge(2)
+    pass_edge(3)
     wait_rim((0, 1, 2, 4))
-    edge_stages((0, 1, 2))
-    lax.fori_loop(0, 3 * heads, first_rim_body, 0)
-
+
+    def first_rim(head):
+        for t in range(3):
+            rim_pairs(t, 0, head)
+
+    over_heads(first_rim, 1)
     load_out_weight.wait()
     load_cached.wait()
     for copies in (to_sibling, to_cross, passed):
         for copy in copies:
             copy.wait_send()
     wait_rim((3, 5, 6, 7))
-    edge_stages((3,))
+    project_edge(3)
 
     @pl.when(left_edge + right_edge == 1)
     def _():
@@ -454,8 +484,7 @@
             edge_pass(stage).wait_send()
 
     pl.semaphore_signal(free_sem, inc=1, device_id=(g, sibling), device_id_type=MESH)
-    second_rim_tile(far_tile)
-    second_rim_tile(1)
+    over_heads(lambda head: rim_pairs(far_tile, 1, head), half_heads)
     pl.semaphore_wait(free_sem, 1)
 
     def partial_sums(first, second):
@@ -503,18 +532,18 @@
         last.append(copy)
 
     for step in range(3):
-        project_out(step, step, 1 - y, step)
-        if step > 0:
-            send_last(step - 1)
-    send_last(2)
-    second_rim_tile(near_tile)
+        project_out(step, step, 1 - y, (1 - y) * (2 - step) + y * step)
+        if step == 0:
+            over_heads(lambda head: rim_pairs(1, 1, head), half_heads)
+        send_last(step)
+    over_heads(lambda head: rim_pairs(near_tile, 1, head), half_heads)
     for step in range(3):
-        project_out(3 + step, step, y, step)
+        project_out(3 + step, step, y, y * (2 - step) + (1 - y) * step)
     stores = []
     for step in range(3):
         sums[3 + step].wait_recv()
         last[step].wait_recv()
-        here = pl.ds(step * chunk, chunk)
+        here = pl.ds(aligned((y * (2 - step) + (1 - y) * step) * chunk), chunk)
         total = (
             rows_buffer[pl.ds((3 + step) * chunk, chunk), :].astype(F32)
             + rim_rows[pl.ds((3 + step) * chunk, chunk), :].astype(F32)

time: 155 us -> 134 us (0.86)
  Pallas kernels: 150 us -> 129 us
    pallas_call x1, Pallas kernels: 150 us -> 129 us  [on_device(): pl.pallas_call(functools.partial(kernel, (groups, heads, tile, width, win...]
where the time goes in v3:
time: 134 us
  Pallas kernels  129 us (96%)
  local copies, waits for them, and re-layouts  4.23 us (3%)
    pallas_call x1, Pallas kernels, on_device(): pl.pallas_call(functools.partial(kernel, (groups, heads, tile, width, win...  129 us
    unnamed x2, local copies, waits for them, and re-layouts  4.23 us

profile of v3, /device:TPU:1, one launch (start us, length us, event | category | flops | bytes accessed | tf_op | source)
XLA Modules:
  0.0 134.0 jit_solution(17559500853559608843)
XLA Ops:
  0.7 1.4 %copy.14.window_tiles_ref = s32[32,3,5]{2,1,0:T(4,128)} copy(s32[32,3,5]{0,1,2:T(4,128)} %param.24) | data formatting | bytes 3840 | tf_op args[11]
  2.1 129.1 %shard_map.127 = bf16[288,3072]{1,0:T(8,128)(2,1)} custom-call(bf16[288,3072]{1,0:T(8,128)(2,1)} %latents_hbm.1, f32[1,3072]{1,0:T(1,128)} %bitcast.5, f32[1,3072]{1,0:T(1,128)} %bitcast.6, f32[1,3072]{1,0:T(1,128)} %bitcast.7, bf16[3072,2304]{1,0:T(8,128)(2,1)} %weight_hbm.1, f32[1,128]{1,0:T(1,128)} %bitcast.8, f32[1,128]{1,0:T(1,128)} %bitcast.9, ...), custom_call_target="tpu_custom_call" | custom-call | tf_op jit(solution)/shard_map/pallas_call | solution.py:594
  131.2 2.8 %copy.17 = bf16[288,3072]{1,0:T(8,128)(2,1)} copy(bf16[288,3072]{1,0:T(8,128)(2,1)} %shard_map.127) | data formatting | bytes 3538944

commit v4 on v3

--- a/solution.py
+++ b/solution.py
@@ -79,6 +79,9 @@
     left_partner = (left, h + left_edge * (cross - h))
     right_partner = (right, h + right_edge * (cross - h))
     edge_side = right_edge
+    first_group = (groups - g) // groups
+    last_group = (g + 1) // groups
+    edge_here = left_edge - first_group + right_edge - last_group
 
     def aligned(start):
         return pl.multiple_of(start, chunk)
@@ -104,9 +107,18 @@
     load_cached = pltpu.make_async_copy(cached_hbm, attended, local_sem.at[5])
 
     barrier = pltpu.get_barrier_semaphore()
-    for partner in ((g, sibling), (g, cross), left_partner, right_partner):
-        pl.semaphore_signal(barrier, inc=1, device_id=partner, device_id_type=MESH)
-    pl.semaphore_wait(barrier, 4)
+    for partner, absent in (
+        ((g, sibling), 0),
+        ((g, cross), 0),
+        (left_partner, first_group),
+        (right_partner, last_group),
+    ):
+
+        @pl.when(absent == 0)
+        def _():
+            pl.semaphore_signal(barrier, inc=1, device_id=partner, device_id_type=MESH)
+
+    pl.semaphore_wait(barrier, 4 - first_group - last_group)
 
     load_latents.wait()
     to_sibling, to_cross = [], []
@@ -145,7 +157,7 @@
         used = [jnp.int32(0)] * 3
         for j in range(3):
             for w in range(window):
-                entry = window_tiles_ref[reader, j, w]
+                entry = window_tiles_ref[w, j, reader]
                 for t in range(3):
                     used[t] = used[t] | (entry == owner * 3 + t).astype(jnp.int32)
         spare = jnp.where(used[1] == 0, 1, jnp.where(used[0] == 0, 0, 2))
@@ -160,7 +172,7 @@
     for j in range(3):
         hits = [jnp.int32(0)] * 7
         for w in range(window):
-            entry = window_tiles_ref[g, j, w]
+            entry = window_tiles_ref[w, j, g]
             inside = (w < window_count_ref[0, j]).astype(jnp.int32)
             for k in range(7):
                 hits[k] = hits[k] + inside * (entry == candidates[k]).astype(jnp.int32)
@@ -275,7 +287,7 @@
         for side in range(2):
             edge = right_edge if side == 0 else left_edge
 
-            @pl.when(edge == 1)
+            @pl.when(edge - (last_group if side == 0 else first_group) == 1)
             def _():
                 second, quarter = (
                     (1 - c) * even + c * odd
@@ -302,14 +314,14 @@
                     tile_copy(side, slot).wait_recv()
 
     def pass_edge(stage):
-        @pl.when(left_edge + right_edge == 1)
+        @pl.when(edge_here == 1)
         def _():
             for half in range(2):
                 edge_copy(edge_side, 2 * stage + half).wait_recv()
             edge_pass(stage).start()
 
     def project_edge(stage):
-        @pl.when(left_edge + right_edge == 1)
+        @pl.when(edge_here == 1)
         def _():
             edge_pass(stage).wait_recv()
             places = []
@@ -381,16 +393,17 @@
         numerator[here, columns] = out
         totals[here, columns] = total
 
-    def rim_pairs(t, phase, head):
+    def rim_pairs(t, phases, head):
         here = pl.ds(aligned(t * tile), tile)
         columns, value_columns = columns_of(head)
         keys, values, names = [], [], []
-        for side in range(2):
-            edge = left_edge if side == 0 else right_edge
-            second = (y + edge + phase) % 2
-            keys.append(rim[side, second, :, columns])
-            values.append(rim[side, second, :, value_columns])
-            names.append(masks[t * 8 + 3 + 2 * side + second])
+        for phase in phases:
+            for side in range(2):
+                edge = left_edge if side == 0 else right_edge
+                second = (y + edge + phase) % 2
+                keys.append(rim[side, second, :, columns])
+                values.append(rim[side, second, :, value_columns])
+                names.append(masks[t * 8 + 3 + 2 * side + second])
         out, total = attend(
             queries[here, columns],
             jnp.concatenate(keys, axis=0),
@@ -398,7 +411,7 @@
             names,
         )
         out, total = numerator[here, columns] + out, totals[here, columns] + total
-        if phase == 0:
+        if 1 not in phases:
             numerator[here, columns] = out
             totals[here, columns] = total
         else:
@@ -407,7 +420,11 @@
                 masks[t * 8 + 7] > 0.5, slot_out, attended[here, columns]
             )
 
-    half_heads = heads // 2
+    triple = math.gcd(heads, 3)
+
+    @pl.when(first_group + last_group == 1)
+    def _():
+        rim[edge_side] = jnp.zeros(rim.shape[1:], BF16)
 
     for load in load_weight:
         load.wait()
@@ -443,33 +460,28 @@
         )
         send_tiles_of(step + 1)
         if step == 0:
-            over_heads(lambda head: own_pairs(near_tile, near_tile, 1, True, head), half_heads)
+            over_heads(lambda head: own_pairs(near_tile, near_tile, 1, True, head), heads)
         if step == 1:
 
             def two_tiles(head):
                 own_pairs(near_tile, 1, 1, False, head)
                 own_pairs(1, y, 2, True, head)
 
-            over_heads(two_tiles, 1)
+            over_heads(two_tiles, 2)
             project_edge(0)
     project_edge(1)
     pass_edge(2)
-
-    def three_tiles(head):
+    over_heads(lambda head: own_pairs(far_tile, 0, 3, True, head), 2)
+
+    def two_singles(head):
         own_pairs(near_tile, far_tile, 1, False, head)
         own_pairs(1, far_tile, 1, False, head)
-        own_pairs(far_tile, 0, 3, True, head)
-
-    over_heads(three_tiles, 1)
+
+    over_heads(two_singles, triple)
     project_edge(2)
     pass_edge(3)
     wait_rim((0, 1, 2, 4))
-
-    def first_rim(head):
-        for t in range(3):
-            rim_pairs(t, 0, head)
-
-    over_heads(first_rim, 1)
+    over_heads(lambda head: rim_pairs(far_tile, (0,), head), heads)
     load_out_weight.wait()
     load_cached.wait()
     for copies in (to_sibling, to_cross, passed):
@@ -478,13 +490,13 @@
     wait_rim((3, 5, 6, 7))
     project_edge(3)
 
-    @pl.when(left_edge + right_edge == 1)
+    @pl.when(edge_here == 1)
     def _():
         for stage in range(4):
             edge_pass(stage).wait_send()
 
     pl.semaphore_signal(free_sem, inc=1, device_id=(g, sibling), device_id_type=MESH)
-    over_heads(lambda head: rim_pairs(far_tile, 1, head), half_heads)
+    over_heads(lambda head: rim_pairs(far_tile, (1,), head), heads)
     pl.semaphore_wait(free_sem, 1)
 
     def partial_sums(first, second):
@@ -534,9 +546,9 @@
     for step in range(3):
         project_out(step, step, 1 - y, (1 - y) * (2 - step) + y * step)
         if step == 0:
-            over_heads(lambda head: rim_pairs(1, 1, head), half_heads)
+            over_heads(lambda head: rim_pairs(1, (0, 1), head), 2)
         send_last(step)
-    over_heads(lambda head: rim_pairs(near_tile, 1, head), half_heads)
+    over_heads(lambda head: rim_pairs(near_tile, (0, 1), head), 2)
     for step in range(3):
         project_out(3 + step, step, y, y * (2 - step) + (1 - y) * step)
     stores = []
@@ -560,8 +572,11 @@
     for copy in sums + last:
         copy.wait_send()
     for side in range(2):
-        for slot in range(8):
-            tile_copy(side, slot).wait_send()
+
+        @pl.when((last_group if side == 0 else first_group) == 0)
+        def _():
+            for slot in range(8):
+                tile_copy(side, slot).wait_send()
 
 
 def on_device(
@@ -657,7 +672,7 @@
         cached,
         active_tiles,
         active_count,
-        window_tiles,
+        window_tiles.transpose(2, 1, 0),
         window_count,
     )
 

time: 134 us -> 126 us (0.940)
  the two profiles are of different devices: /device:TPU:1 before, /device:TPU:104 now
where the time goes in v4:
time: 126 us; the launch traced here: 125 us
  Pallas kernels  121 us (96%)
  local copies, waits for them, and re-layouts  2.8 us (2%)
    pallas_call x1, Pallas kernels, on_device(): pl.pallas_call(functools.partial(kernel, (groups, heads, tile, width, win...  121 us
    unnamed x1, local copies, waits for them, and re-layouts  2.8 us

profile of v4, /device:TPU:104, one launch (start us, length us, event | category | flops | bytes accessed | tf_op | source)
XLA Modules:
  0.0 124.6 jit_solution(16392706085037669414)
XLA Ops:
  0.7 121.2 %shard_map.127 = bf16[288,3072]{1,0:T(8,128)(2,1)} custom-call(bf16[288,3072]{1,0:T(8,128)(2,1)} %latents_hbm.1, f32[1,3072]{1,0:T(1,128)} %bitcast.6, f32[1,3072]{1,0:T(1,128)} %bitcast.7, f32[1,3072]{1,0:T(1,128)} %bitcast.8, bf16[3072,2304]{1,0:T(8,128)(2,1)} %weight_hbm.1, f32[1,128]{1,0:T(1,128)} %bitcast.10, f32[1,128]{1,0:T(1,128)} %bitcast.11, ...), custom_call_target="tpu_custom_call" | custom-call | tf_op jit(solution)/shard_map/pallas_call | solution.py:609
  121.8 2.8 %copy.16 = bf16[288,3072]{1,0:T(8,128)(2,1)} copy(bf16[288,3072]{1,0:T(8,128)(2,1)} %shard_map.127) | data formatting | bytes 3538944

commit v5 on v4

--- a/solution.py
+++ b/solution.py
@@ -54,6 +54,8 @@
     pass_recv,
     rim_send_sem,
     rim_recv_sem,
+    rim_first_send,
+    rim_first_recv,
     rim_pass_send,
     rim_pass_recv,
     sums_send,
@@ -118,10 +120,8 @@
         def _():
             pl.semaphore_signal(barrier, inc=1, device_id=partner, device_id_type=MESH)
 
-    pl.semaphore_wait(barrier, 4 - first_group - last_group)
-
     load_latents.wait()
-    to_sibling, to_cross = [], []
+    mine_at = []
     for step in range(3):
         mine = (1 - y) * (2 - step) + y * step
         x = latents[pl.ds(aligned(mine * chunk), chunk), :].astype(F32)
@@ -130,10 +130,15 @@
         normed = (
             centred * lax.rsqrt(variance + 1e-06) * (1.0 + scale_ref[...]) + shift_ref[...]
         ).astype(BF16)
-        place = aligned(c * rows + mine * chunk)
-        rows_buffer[pl.ds(place, chunk), :] = normed
+        place = pl.ds(aligned(c * rows + mine * chunk), chunk)
+        rows_buffer[place, :] = normed
+        mine_at.append(place)
+
+    pl.semaphore_wait(barrier, 4 - first_group - last_group)
+    to_sibling, to_cross = [], []
+    for step, place in enumerate(mine_at):
         over = pltpu.make_async_remote_copy(
-            src_ref=rows_buffer.at[pl.ds(place, chunk), :],
+            src_ref=rows_buffer.at[place, :],
             dst_ref=rows_buffer.at[pl.ds(far_place(step, c), chunk), :],
             send_sem=cross_send.at[step],
             recv_sem=cross_recv.at[step],
@@ -143,8 +148,8 @@
         over.start()
         to_cross.append(over)
         beside = pltpu.make_async_remote_copy(
-            src_ref=rows_buffer.at[pl.ds(place, chunk), :],
-            dst_ref=rows_buffer.at[pl.ds(place, chunk), :],
+            src_ref=rows_buffer.at[place, :],
+            dst_ref=rows_buffer.at[place, :],
             send_sem=near_sib_send.at[step],
             recv_sem=near_sib_recv.at[step],
             device_id=(g, sibling),
@@ -191,23 +196,33 @@
         return (vectors * lax.rsqrt(mean_square + 1e-06) * gain_ref[...]).astype(BF16)
 
     pair = 2 * 3 * HD
-
-    def project(block_at, places):
+    bank_pair = 4 * HD
+
+    def columns_of(head):
+        at = head // 2 * bank_pair + head % 2 * HD
+        return (
+            pl.ds(pl.multiple_of(head * HD, HD), HD),
+            pl.ds(pl.multiple_of(at, HD), HD),
+            pl.ds(pl.multiple_of(at + 2 * HD, HD), HD),
+        )
+
+    def project(block_at, places, after=None):
         def body(step, carry):
             columns = pl.ds(pl.multiple_of(step * pair, pair), pair)
             packed = jnp.dot(rows_buffer[block_at, :], weight[:, columns], preferred_element_type=F32)
             for half in range(2):
                 at = half * 3 * HD
                 head = step * 2 + half
-                query_columns = pl.ds(pl.multiple_of(head * HD, HD), HD)
-                value_columns = pl.ds(pl.multiple_of(share + head * HD, HD), HD)
+                query_columns, key_columns, value_columns = columns_of(head)
                 q = head_norm(packed[:, at : at + HD], query_gain_ref)
                 k = head_norm(packed[:, at + HD : at + 2 * HD], key_gain_ref)
                 v = packed[:, at + 2 * HD : at + 3 * HD].astype(BF16)
                 for first, place, count in places:
                     queries[pl.ds(place, count), query_columns] = q[first : first + count]
-                    bank[pl.ds(place, count), query_columns] = k[first : first + count]
+                    bank[pl.ds(place, count), key_columns] = k[first : first + count]
                     bank[pl.ds(place, count), value_columns] = v[first : first + count]
+            if after is not None:
+                after(step)
             return carry
 
         lax.fori_loop(0, heads // 2, body, 0)
@@ -269,6 +284,34 @@
     def takes_high(side, second):
         first_tile, second_tile = send_tiles[side]
         return jnp.where(second == 0, first_tile, second_tile - 1) == 1
+
+    def first_copy(side, slot, step):
+        second, quarter = quarter_of(slot, y)
+        columns = pl.ds(pl.multiple_of(step * bank_pair, bank_pair), bank_pair)
+        return pltpu.make_async_remote_copy(
+            src_ref=rim_send.at[side, slot, :, columns],
+            dst_ref=rim.at[side, second, pl.ds(aligned(quarter * chunk), chunk), columns],
+            send_sem=rim_first_send.at[side, slot, step],
+            recv_sem=rim_first_recv.at[side, slot, step],
+            device_id=(right if side == 0 else left, h),
+            device_id_type=MESH,
+        )
+
+    def send_first_tiles(step):
+        columns = pl.ds(pl.multiple_of(step * bank_pair, bank_pair), bank_pair)
+        for side in range(2):
+            edge = right_edge if side == 0 else left_edge
+
+            @pl.when(edge == 0)
+            def _():
+                for slot in range(2):
+                    second, quarter = quarter_of(slot, y)
+                    low = pl.ds(aligned((4 * second + quarter) * chunk), chunk)
+                    high = pl.ds(aligned((4 * second + quarter + 4) * chunk), chunk)
+                    rim_send[side, slot, :, columns] = jnp.where(
+                        takes_high(side, second), bank[high, columns], bank[low, columns]
+                    )
+                    first_copy(side, slot, step).start()
 
     def send_tiles_of(stage):
         for side in range(2):
@@ -311,7 +354,11 @@
             @pl.when(edge == 0)
             def _():
                 for slot in slots:
-                    tile_copy(side, slot).wait_recv()
+                    if slot < 2:
+                        for step in range(heads // 2):
+                            first_copy(side, slot, step).wait_recv()
+                    else:
+                        tile_copy(side, slot).wait_recv()
 
     def pass_edge(stage):
         @pl.when(edge_here == 1)
@@ -339,8 +386,7 @@
                     )
                     k = head_norm(packed[:, :HD], key_gain_ref)
                     v = packed[:, HD:].astype(BF16)
-                    key_columns = pl.ds(pl.multiple_of(head * HD, HD), HD)
-                    value_columns = pl.ds(pl.multiple_of(share + head * HD, HD), HD)
+                    _, key_columns, value_columns = columns_of(head)
                     for first, second, place in places:
                         there = pl.ds(place, chunk)
                         rim[edge_side, second, there, key_columns] = k[first : first + chunk]
@@ -350,6 +396,7 @@
             lax.fori_loop(0, heads // 2, body, 0)
 
     log_scale = math.log2(math.e) / math.sqrt(HD)
+    triple = math.gcd(heads, 3)
     near_tile = y * 2
     far_tile = (1 - y) * 2
 
@@ -364,12 +411,6 @@
             total = total + weights[:, at : at + HD]
         return jnp.dot(weights.astype(BF16), values, preferred_element_type=F32), total
 
-    def columns_of(head):
-        return (
-            pl.ds(pl.multiple_of(head * HD, HD), HD),
-            pl.ds(pl.multiple_of(share + head * HD, HD), HD),
-        )
-
     def over_heads(work, unroll):
         def body(step, carry):
             for inner in range(unroll):
@@ -378,39 +419,30 @@
 
         lax.fori_loop(0, heads // unroll, body, 0)
 
-    def own_pairs(t, first_key, count, fresh, head):
+    def tile_pairs(t, own, phases, fresh, head):
         here = pl.ds(aligned(t * tile), tile)
-        there = pl.ds(aligned(first_key * tile), count * tile)
-        columns, value_columns = columns_of(head)
-        out, total = attend(
-            queries[here, columns],
-            bank[there, columns],
-            bank[there, value_columns],
-            [masks[t * 8 + first_key + k] for k in range(count)],
-        )
-        if not fresh:
-            out, total = numerator[here, columns] + out, totals[here, columns] + total
-        numerator[here, columns] = out
-        totals[here, columns] = total
-
-    def rim_pairs(t, phases, head):
-        here = pl.ds(aligned(t * tile), tile)
-        columns, value_columns = columns_of(head)
+        columns, key_columns, value_columns = columns_of(head)
         keys, values, names = [], [], []
+        for first, count in own:
+            there = pl.ds(aligned(first * tile), count * tile)
+            keys.append(bank[there, key_columns])
+            values.append(bank[there, value_columns])
+            names += [masks[t * 8 + first + k] for k in range(count)]
         for phase in phases:
             for side in range(2):
                 edge = left_edge if side == 0 else right_edge
                 second = (y + edge + phase) % 2
-                keys.append(rim[side, second, :, columns])
+                keys.append(rim[side, second, :, key_columns])
                 values.append(rim[side, second, :, value_columns])
                 names.append(masks[t * 8 + 3 + 2 * side + second])
         out, total = attend(
             queries[here, columns],
-            jnp.concatenate(keys, axis=0),
-            jnp.concatenate(values, axis=0),
+            jnp.concatenate(keys, axis=0) if len(keys) > 1 else keys[0],
+            jnp.concatenate(values, axis=0) if len(values) > 1 else values[0],
             names,
         )
-        out, total = numerator[here, columns] + out, totals[here, columns] + total
+        if not fresh:
+            out, total = numerator[here, columns] + out, totals[here, columns] + total
         if 1 not in phases:
             numerator[here, columns] = out
             totals[here, columns] = total
@@ -420,8 +452,6 @@
                 masks[t * 8 + 7] > 0.5, slot_out, attended[here, columns]
             )
 
-    triple = math.gcd(heads, 3)
-
     @pl.when(first_group + last_group == 1)
     def _():
         rim[edge_side] = jnp.zeros(rim.shape[1:], BF16)
@@ -433,8 +463,9 @@
     for copy in to_sibling:
         copy.wait_recv()
     send_rows_of(0)
-    project(pl.ds(0, 2 * rows), [(0, aligned(y * 2 * rows), 2 * rows)])
-    send_tiles_of(0)
+    project(
+        pl.ds(0, 2 * rows), [(0, aligned(y * 2 * rows), 2 * rows)], after=send_first_tiles
+    )
     passed = []
     for step in range(3):
         to_cross[step].wait_recv()
@@ -450,8 +481,6 @@
         passed.append(onward)
         onward.wait_recv()
         send_rows_of(step + 1)
-        if step > 0:
-            pass_edge(step - 1)
         theirs = y * (2 - step) + (1 - y) * step
         start = (1 - y) * 2 * rows + theirs * chunk
         project(
@@ -459,29 +488,17 @@
             [(0, aligned(start), chunk), (chunk, aligned(start + rows), chunk)],
         )
         send_tiles_of(step + 1)
+        pass_edge(step)
         if step == 0:
-            over_heads(lambda head: own_pairs(near_tile, near_tile, 1, True, head), heads)
-        if step == 1:
-
-            def two_tiles(head):
-                own_pairs(near_tile, 1, 1, False, head)
-                own_pairs(1, y, 2, True, head)
-
-            over_heads(two_tiles, 2)
-            project_edge(0)
-    project_edge(1)
-    pass_edge(2)
-    over_heads(lambda head: own_pairs(far_tile, 0, 3, True, head), 2)
-
-    def two_singles(head):
-        own_pairs(near_tile, far_tile, 1, False, head)
-        own_pairs(1, far_tile, 1, False, head)
-
-    over_heads(two_singles, triple)
-    project_edge(2)
+            over_heads(lambda head: tile_pairs(near_tile, [(near_tile, 1)], (), True, head), heads)
+        elif step == 1:
+            over_heads(lambda head: tile_pairs(1, [(y, 2)], (), True, head), triple)
+        else:
+            over_heads(lambda head: tile_pairs(far_tile, [(0, 3)], (), True, head), 2)
+        project_edge(step)
     pass_edge(3)
     wait_rim((0, 1, 2, 4))
-    over_heads(lambda head: rim_pairs(far_tile, (0,), head), heads)
+    over_heads(lambda head: tile_pairs(far_tile, [], (0,), False, head), heads)
     load_out_weight.wait()
     load_cached.wait()
     for copies in (to_sibling, to_cross, passed):
@@ -496,7 +513,7 @@
             edge_pass(stage).wait_send()
 
     pl.semaphore_signal(free_sem, inc=1, device_id=(g, sibling), device_id_type=MESH)
-    over_heads(lambda head: rim_pairs(far_tile, (1,), head), heads)
+    over_heads(lambda head: tile_pairs(far_tile, [], (1,), False, head), heads)
     pl.semaphore_wait(free_sem, 1)
 
     def partial_sums(first, second):
@@ -546,9 +563,13 @@
     for step in range(3):
         project_out(step, step, 1 - y, (1 - y) * (2 - step) + y * step)
         if step == 0:
-            over_heads(lambda head: rim_pairs(1, (0, 1), head), 2)
+            over_heads(
+                lambda head: tile_pairs(1, [(far_tile, 1)], (0, 1), False, head), 2
+            )
         send_last(step)
-    over_heads(lambda head: rim_pairs(near_tile, (0, 1), head), 2)
+    over_heads(
+        lambda head: tile_pairs(near_tile, [(1, 1), (far_tile, 1)], (0, 1), False, head), 2
+    )
     for step in range(3):
         project_out(3 + step, step, y, y * (2 - step) + (1 - y) * step)
     stores = []
@@ -575,8 +596,21 @@
 
         @pl.when((last_group if side == 0 else first_group) == 0)
         def _():
-            for slot in range(8):
+            for slot in range(2, 8):
                 tile_copy(side, slot).wait_send()
+
+        edge = right_edge if side == 0 else left_edge
+
+        @pl.when(edge == 0)
+        def _():
+            for slot in range(2):
+                for step in range(heads // 2):
+                    first_copy(side, slot, step).wait_send()
+
+        @pl.when(edge - (last_group if side == 0 else first_group) == 1)
+        def _():
+            for slot in range(2):
+                edge_copy(side, slot).wait_send()
 
 
 def on_device(
@@ -649,6 +683,8 @@
             dma((3,)),
             dma((2, 8)),
             dma((2, 8)),
+            dma((2, 2, heads // 2)),
+            dma((2, 2, heads // 2)),
             dma((4,)),
             dma((4,)),
             dma((6,)),

time: 126 us -> 123 us (0.976)
  Pallas kernels: 121 us -> 119 us
    pallas_call x1, Pallas kernels: 121 us -> 119 us  [on_device(): pl.pallas_call(functools.partial(kernel, (groups, heads, tile, width, win...]
where the time goes in v5:
time: 123 us
  Pallas kernels  119 us (97%)
  local copies, waits for them, and re-layouts  2.8 us (2%)
    pallas_call x1, Pallas kernels, on_device(): pl.pallas_call(functools.partial(kernel, (groups, heads, tile, width, win...  119 us
    unnamed x1, local copies, waits for them, and re-layouts  2.8 us

profile of v5, /device:TPU:104, one launch (start us, length us, event | category | flops | bytes accessed | tf_op | source)
XLA Modules:
  0.0 122.5 jit_solution(8435088978461306732)
XLA Ops:
  0.7 119.0 %shard_map.127 = bf16[288,3072]{1,0:T(8,128)(2,1)} custom-call(bf16[288,3072]{1,0:T(8,128)(2,1)} %latents_hbm.1, f32[1,3072]{1,0:T(1,128)} %bitcast.6, f32[1,3072]{1,0:T(1,128)} %bitcast.7, f32[1,3072]{1,0:T(1,128)} %bitcast.8, bf16[3072,2304]{1,0:T(8,128)(2,1)} %weight_hbm.1, f32[1,128]{1,0:T(1,128)} %bitcast.10, f32[1,128]{1,0:T(1,128)} %bitcast.11, ...), custom_call_target="tpu_custom_call" | custom-call | tf_op jit(solution)/shard_map/pallas_call | solution.py:643
  119.7 2.8 %copy.16 = bf16[288,3072]{1,0:T(8,128)(2,1)} copy(bf16[288,3072]{1,0:T(8,128)(2,1)} %shard_map.127) | data formatting | bytes 3538944

commit v6 on v5

--- a/solution.py
+++ b/solution.py
@@ -516,57 +516,68 @@
     over_heads(lambda head: tile_pairs(far_tile, [], (1,), False, head), heads)
     pl.semaphore_wait(free_sem, 1)
 
-    def partial_sums(first, second):
-        both = jnp.concatenate(
-            [attended[pl.ds(aligned(first), chunk), :], attended[pl.ds(aligned(second), chunk), :]],
-            axis=0,
-        )
-        return jnp.dot(both, out_weight[...], preferred_element_type=F32).astype(BF16)
-
-    sums = []
+    def half_columns(half):
+        return pl.ds(half * half_width, half_width)
+
+    sums = {}
 
     def project_out(slot, step, chip, chunk_at):
         owner = chip * 2 * rows + chunk_at * chunk
-        both = partial_sums(owner + c * rows, owner + (1 - c) * rows)
-        half = slot // 3
-        rows_buffer[pl.ds((3 * half + step) * chunk, chunk), :] = both[:chunk]
-        rows_buffer[pl.ds((6 + slot) * chunk, chunk), :] = both[chunk:]
-        copy = pltpu.make_async_remote_copy(
-            src_ref=rows_buffer.at[pl.ds((6 + slot) * chunk, chunk), :],
-            dst_ref=rim_rows.at[pl.ds(slot * chunk, chunk), :],
-            send_sem=sums_send.at[slot],
-            recv_sem=sums_recv.at[slot],
-            device_id=(g, sibling),
-            device_id_type=MESH,
-        )
-        copy.start()
-        sums.append(copy)
-
-    last = []
+        both = jnp.concatenate(
+            [
+                attended[pl.ds(aligned(owner + core * rows), chunk), :]
+                for core in (c, 1 - c)
+            ],
+            axis=0,
+        )
+        kept = pl.ds((3 * (slot // 3) + step) * chunk, chunk)
+        given = pl.ds((6 + slot) * chunk, chunk)
+        for half in range(2):
+            columns = half_columns(half)
+            part = jnp.dot(both, out_weight[:, columns], preferred_element_type=F32).astype(BF16)
+            rows_buffer[given, columns] = part[chunk:]
+            copy = pltpu.make_async_remote_copy(
+                src_ref=rows_buffer.at[given, columns],
+                dst_ref=rim_rows.at[pl.ds(slot * chunk, chunk), columns],
+                send_sem=sums_send.at[slot, half],
+                recv_sem=sums_recv.at[slot, half],
+                device_id=(g, sibling),
+                device_id_type=MESH,
+            )
+            copy.start()
+            sums[slot, half] = copy
+            rows_buffer[kept, columns] = part[:chunk]
+
+    last = {}
 
     def send_last(step):
-        sums[step].wait_recv()
         here = pl.ds(step * chunk, chunk)
-        kept = rows_buffer[here, :].astype(F32)
-        rows_buffer[here, :] = (kept + rim_rows[here, :].astype(F32)).astype(BF16)
-        copy = pltpu.make_async_remote_copy(
-            src_ref=rows_buffer.at[pl.ds(step * chunk, chunk), :],
-            dst_ref=cross_sums.at[step],
-            send_sem=last_send.at[step],
-            recv_sem=last_recv.at[step],
-            device_id=(g, cross),
-            device_id_type=MESH,
-        )
-        copy.start()
-        last.append(copy)
-
-    for step in range(3):
+        for half in range(2):
+            columns = half_columns(half)
+            sums[step, half].wait_recv()
+            kept = rows_buffer[here, columns].astype(F32)
+            rows_buffer[here, columns] = (kept + rim_rows[here, columns].astype(F32)).astype(BF16)
+            copy = pltpu.make_async_remote_copy(
+                src_ref=rows_buffer.at[here, columns],
+                dst_ref=cross_sums.at[step, :, columns],
+                send_sem=last_send.at[step, half],
+                recv_sem=last_recv.at[step, half],
+                device_id=(g, cross),
+                device_id_type=MESH,
+            )
+            copy.start()
+            last[step, half] = copy
+
+    def far_out(step):
         project_out(step, step, 1 - y, (1 - y) * (2 - step) + y * step)
-        if step == 0:
-            over_heads(
-                lambda head: tile_pairs(1, [(far_tile, 1)], (0, 1), False, head), 2
-            )
-        send_last(step)
+
+    far_out(0)
+    send_last(0)
+    over_heads(lambda head: tile_pairs(1, [(far_tile, 1)], (0, 1), False, head), 2)
+    far_out(1)
+    far_out(2)
+    send_last(1)
+    send_last(2)
     over_heads(
         lambda head: tile_pairs(near_tile, [(1, 1), (far_tile, 1)], (0, 1), False, head), 2
     )
@@ -574,24 +585,29 @@
         project_out(3 + step, step, y, y * (2 - step) + (1 - y) * step)
     stores = []
     for step in range(3):
-        sums[3 + step].wait_recv()
-        last[step].wait_recv()
         here = pl.ds(aligned((y * (2 - step) + (1 - y) * step) * chunk), chunk)
-        total = (
-            rows_buffer[pl.ds((3 + step) * chunk, chunk), :].astype(F32)
-            + rim_rows[pl.ds((3 + step) * chunk, chunk), :].astype(F32)
-            + cross_sums[step].astype(F32)
-        )
-        latents[here, :] = (latents[here, :].astype(F32) + gate_ref[...] * total).astype(BF16)
-        store = pltpu.make_async_copy(
-            latents.at[here, :], out_hbm.at[here, :], local_sem.at[step]
-        )
-        store.start()
-        stores.append(store)
+        own = pl.ds((3 + step) * chunk, chunk)
+        for half in range(2):
+            columns = half_columns(half)
+            sums[3 + step, half].wait_recv()
+            near_sum = rows_buffer[own, columns].astype(F32) + rim_rows[own, columns].astype(F32)
+            last[step, half].wait_recv()
+            total = near_sum + cross_sums[step, :, columns].astype(F32)
+            latents[here, columns] = (
+                latents[here, columns].astype(F32) + gate_ref[:, columns] * total
+            ).astype(BF16)
+            store = pltpu.make_async_copy(
+                latents.at[here, columns],
+                out_hbm.at[here, columns],
+                local_sem.at[2 * step + half],
+            )
+            store.start()
+            stores.append(store)
     for store in stores:
         store.wait()
-    for copy in sums + last:
-        copy.wait_send()
+    for copies in (sums, last):
+        for copy in copies.values():
+            copy.wait_send()
     for side in range(2):
 
         @pl.when((last_group if side == 0 else first_group) == 0)
@@ -687,10 +703,10 @@
             dma((2, 2, heads // 2)),
             dma((4,)),
             dma((4,)),
-            dma((6,)),
-            dma((6,)),
-            dma((3,)),
-            dma((3,)),
+            dma((6, 2)),
+            dma((6, 2)),
+            dma((3, 2)),
+            dma((3, 2)),
             pltpu.SemaphoreType.REGULAR,
         ],
         compiler_params=pltpu.CompilerParams(

time: 123 us -> 118 us (0.959)
  Pallas kernels: 119 us -> 114 us
    pallas_call x1, Pallas kernels: 119 us -> 114 us  [on_device(): pl.pallas_call(functools.partial(kernel, (groups, heads, tile, width, win...]
where the time goes in v6:
time: 118 us; the launch traced here: 117 us
  Pallas kernels  114 us (97%)
  local copies, waits for them, and re-layouts  2.8 us (2%)
    pallas_call x1, Pallas kernels, on_device(): pl.pallas_call(functools.partial(kernel, (groups, heads, tile, width, win...  114 us
    unnamed x1, local copies, waits for them, and re-layouts  2.8 us

profile of v6, /device:TPU:104, one launch (start us, length us, event | category | flops | bytes accessed | tf_op | source)
XLA Modules:
  0.0 117.4 jit_solution(13576166884479566107)
XLA Ops:
  0.7 113.9 %shard_map.127 = bf16[288,3072]{1,0:T(8,128)(2,1)} custom-call(bf16[288,3072]{1,0:T(8,128)(2,1)} %latents_hbm.1, f32[1,3072]{1,0:T(1,128)} %bitcast.6, f32[1,3072]{1,0:T(1,128)} %bitcast.7, f32[1,3072]{1,0:T(1,128)} %bitcast.8, bf16[3072,2304]{1,0:T(8,128)(2,1)} %weight_hbm.1, f32[1,128]{1,0:T(1,128)} %bitcast.10, f32[1,128]{1,0:T(1,128)} %bitcast.11, ...), custom_call_target="tpu_custom_call" | custom-call | tf_op jit(solution)/shard_map/pallas_call | solution.py:659
  114.6 2.8 %copy.16 = bf16[288,3072]{1,0:T(8,128)(2,1)} copy(bf16[288,3072]{1,0:T(8,128)(2,1)} %shard_map.127) | data formatting | bytes 3538944

commit v7 on v6

--- a/solution.py
+++ b/solution.py
@@ -419,8 +419,25 @@
 
         lax.fori_loop(0, heads // unroll, body, 0)
 
-    def tile_pairs(t, own, phases, fresh, head):
-        here = pl.ds(aligned(t * tile), tile)
+    def tile_pairs(t, own, phases, fresh, head, part=None):
+        start = t * tile
+        if part is None:
+            pieces = [pl.ds(aligned(start), tile)]
+        elif part == 0:
+            pieces = [pl.ds(aligned(start + at * chunk), chunk) for at in (0, 3)]
+        else:
+            pieces = [pl.ds(aligned(start + chunk), 2 * chunk)]
+
+        def load(ref, columns):
+            blocks = [ref[piece, columns] for piece in pieces]
+            return jnp.concatenate(blocks, axis=0) if len(blocks) > 1 else blocks[0]
+
+        def store(ref, columns, value):
+            at = 0
+            for piece in pieces:
+                ref[piece, columns] = value[at : at + piece.size]
+                at += piece.size
+
         columns, key_columns, value_columns = columns_of(head)
         keys, values, names = [], [], []
         for first, count in own:
@@ -436,21 +453,21 @@
                 values.append(rim[side, second, :, value_columns])
                 names.append(masks[t * 8 + 3 + 2 * side + second])
         out, total = attend(
-            queries[here, columns],
+            load(queries, columns),
             jnp.concatenate(keys, axis=0) if len(keys) > 1 else keys[0],
             jnp.concatenate(values, axis=0) if len(values) > 1 else values[0],
             names,
         )
         if not fresh:
-            out, total = numerator[here, columns] + out, totals[here, columns] + total
+            out = load(numerator, columns) + out
+            total = load(totals, columns) + total
         if 1 not in phases:
-            numerator[here, columns] = out
-            totals[here, columns] = total
+            store(numerator, columns, out)
+            store(totals, columns, total)
         else:
             slot_out = (out / jnp.sum(total, axis=-1, keepdims=True)).astype(BF16)
-            attended[here, columns] = jnp.where(
-                masks[t * 8 + 7] > 0.5, slot_out, attended[here, columns]
-            )
+            kept = load(attended, columns)
+            store(attended, columns, jnp.where(masks[t * 8 + 7] > 0.5, slot_out, kept))
 
     @pl.when(first_group + last_group == 1)
     def _():
@@ -496,9 +513,9 @@
         else:
             over_heads(lambda head: tile_pairs(far_tile, [(0, 3)], (), True, head), 2)
         project_edge(step)
+    wait_rim((0, 1, 2, 4))
+    over_heads(lambda head: tile_pairs(far_tile, [], (0,), False, head, 0), heads)
     pass_edge(3)
-    wait_rim((0, 1, 2, 4))
-    over_heads(lambda head: tile_pairs(far_tile, [], (0,), False, head), heads)
     load_out_weight.wait()
     load_cached.wait()
     for copies in (to_sibling, to_cross, passed):
@@ -513,7 +530,7 @@
             edge_pass(stage).wait_send()
 
     pl.semaphore_signal(free_sem, inc=1, device_id=(g, sibling), device_id_type=MESH)
-    over_heads(lambda head: tile_pairs(far_tile, [], (1,), False, head), heads)
+    over_heads(lambda head: tile_pairs(far_tile, [], (1,), False, head, 0), heads)
     pl.semaphore_wait(free_sem, 1)
 
     def half_columns(half):
@@ -573,6 +590,7 @@
 
     far_out(0)
     send_last(0)
+    over_heads(lambda head: tile_pairs(far_tile, [], (0, 1), False, head, 1), triple)
     over_heads(lambda head: tile_pairs(1, [(far_tile, 1)], (0, 1), False, head), 2)
     far_out(1)
     far_out(2)

time: 118 us -> 117 us (level)
  no operation moved by 1% of the time
where the time goes in v7:
time: 117 us; the launch traced here: 116 us
  Pallas kernels  113 us (97%)
  local copies, waits for them, and re-layouts  2.8 us (2%)
    pallas_call x1, Pallas kernels, on_device(): pl.pallas_call(functools.partial(kernel, (groups, heads, tile, width, win...  113 us
    unnamed x1, local copies, waits for them, and re-layouts  2.8 us

profile of v7, /device:TPU:104, one launch (start us, length us, event | category | flops | bytes accessed | tf_op | source)
XLA Modules:
  0.0 116.5 jit_solution(17143870465396316661)
XLA Ops:
  0.7 113.0 %shard_map.127 = bf16[288,3072]{1,0:T(8,128)(2,1)} custom-call(bf16[288,3072]{1,0:T(8,128)(2,1)} %latents_hbm.1, f32[1,3072]{1,0:T(1,128)} %bitcast.6, f32[1,3072]{1,0:T(1,128)} %bitcast.7, f32[1,3072]{1,0:T(1,128)} %bitcast.8, bf16[3072,2304]{1,0:T(8,128)(2,1)} %weight_hbm.1, f32[1,128]{1,0:T(1,128)} %bitcast.10, f32[1,128]{1,0:T(1,128)} %bitcast.11, ...), custom_call_target="tpu_custom_call" | custom-call | tf_op jit(solution)/shard_map/pallas_call | solution.py:677
  113.7 2.8 %copy.16 = bf16[288,3072]{1,0:T(8,128)(2,1)} copy(bf16[288,3072]{1,0:T(8,128)(2,1)} %shard_map.127) | data formatting | bytes 3538944
